TPU v7x, 256 devices: a whole 4x4x8 slice. The times are simulated.
256 devices in a mesh: attn: 8 (over z_lo, core), ffn: 16 (over x, y), rep: 2 (over z_hi).
Axes of the slice: x: 4, y: 4, z: 8 (z_hi: 2, z_lo: 4; z = z_hi * 4 + z_lo), core: 2. Of those that a mesh axis runs over, the one named last changes fastest.
Arguments:
- hidden_in: bfloat16 [3, 256, 7168], P(None, 'rep', 'attn'), parts along dimension 1, may hold values from -18 to 18
- queries: bfloat16 [3, 256, 16384], P(None, ('rep', 'attn', 'ffn')), parts along dimension 1, may hold values from -128 to 128
- key_cache: bfloat16 [768, 1024, 256], P(('rep', 'attn', 'ffn')), parts along dimension 0, may hold values from -6 to 6
- value_cache: bfloat16 [768, 1024, 256], P(('rep', 'attn', 'ffn')), parts along dimension 0, may hold values from -6 to 6
- lengths: int32 [3, 256], P(None, ('rep', 'attn', 'ffn')), parts along dimension 1, may hold values from 256 to 1024, as said below
- cache_slot: int32 [3, 256], P(None, ('rep', 'attn', 'ffn')), parts along dimension 1, may hold values from 0 to 2, as said below
- out_weight: bfloat16 [16384, 7168], P('ffn', 'attn'), may hold values from -0.046875 to 0.046875
- ffn_gain: bfloat16 [7168], P('attn'), may hold values from 0.099609375 to 1.8984375
- gate_weight: bfloat16 [7168, 18432], P('attn', 'ffn'), may hold values from -0.0625 to 0.0625
- up_weight: bfloat16 [7168, 18432], P('attn', 'ffn'), may hold values from -0.0625 to 0.0625
- down_weight: bfloat16 [18432, 7168], P('ffn', 'attn'), may hold values from -0.046875 to 0.046875
Outputs:
- hidden_out: bfloat16 [3, 256, 7168], P(None, ('rep', 'attn', 'ffn')), parts along dimension 1
There are 2 independent parts, one for each index of `rep`. A program takes and returns all parts, laid end to end along the dimension named above; an argument that names none is the same for every part. Nothing has to cross between parts.
Inputs may be any that keep to these rules, and one draw needn't show every extreme that they name: Each request reads positions 0 to lengths - 1 of its slot; request 0 of every micro-batch has a full cache of 1024 positions. `cache_slot`: the requests of one device, over all micro-batches, occupy distinct slots of that device.
All inputs are finite; a program needn't handle non-finite values.
Results may differ from a plain program's by a relative error of at most 0.013.
Values may be sent and summed in bfloat16 or wider, within the bound.
No kernel may reach another device: no remote copies, remote signals or barrier semaphores. Data moves between devices by JAX's collectives and lax.ppermute only.
A program may use at most 64 MiB of HBM per device.

v0:
```python
import functools

import jax
import jax.numpy as jnp
from jax import lax
from jax.experimental import pallas as pl
from jax.experimental.pallas import tpu as pltpu
from jax.sharding import Mesh, PartitionSpec as P

EPSILON = 1e-06
MASKED = -1e30
Z = "z"
CORE = "core"
ATTN = (Z, CORE)
FFN = ("x", "y")
REP = "rep"
LANES = 128
SQ_ROWS = 16
FEW = 16
BF16 = jnp.bfloat16
F32 = jnp.float32
HEAVY = pl.CostEstimate(flops=10**10, bytes_accessed=10**7, transcendentals=0)


def whole():
    return pl.BlockSpec(memory_space=pltpu.VMEM)


def scalars():
    return pl.BlockSpec(memory_space=pltpu.SMEM)


def in_hbm():
    return pl.BlockSpec(memory_space=pltpu.HBM)


def params(mib):
    return pltpu.CompilerParams(vmem_limit_bytes=mib * 1024 * 1024)


def one_hot(shape, source_of_row):
    rows = lax.broadcasted_iota(jnp.int32, (shape[0], 1), 0)
    cols = lax.broadcasted_iota(jnp.int32, shape, 1)
    return jnp.where(cols == source_of_row(rows), 1.0, 0.0)


def attention_kernel(
    slot_hbm,
    length_hbm,
    query_hbm,
    key_hbm,
    value_hbm,
    out_ref,
    slots,
    lengths,
    queries,
    keys,
    values,
    wide,
    small_sem,
    key_sem,
    value_sem,
):
    slot_count, pos, head_dim = keys.shape
    micro, width = queries.shape
    heads = width // head_dim
    copies, blocks, _, tile_rows, _ = out_ref.shape
    small = [
        pltpu.make_async_copy(source, target, small_sem.at[i])
        for i, (source, target) in enumerate(((query_hbm, queries), (slot_hbm, slots), (length_hbm, lengths)))
    ]
    key_copies = [pltpu.make_async_copy(key_hbm.at[s], keys.at[s], key_sem.at[s]) for s in range(slot_count)]
    value_copies = [pltpu.make_async_copy(value_hbm.at[s], values.at[s], value_sem.at[s]) for s in range(slot_count)]
    for copy in small + key_copies + value_copies:
        copy.start()
    for copy in small:
        copy.wait()
    for h in range(heads):
        wide[:, h, :] = queries[:, h * head_dim : (h + 1) * head_dim].astype(F32)
    pieces = head_dim // LANES
    group = heads // blocks
    positions = lax.broadcasted_iota(jnp.int32, (heads, pos), 1)
    softened = []
    totals = []
    for copy in key_copies:
        copy.wait()
    for m in range(micro):
        scores = lax.dot_general(
            wide[m].astype(BF16), keys[slots[0, m]], (((1,), (1,)), ((), ())), preferred_element_type=F32
        ) * head_dim ** (-0.5)
        in_cache = positions < lengths[0, m]
        scores = jnp.where(in_cache, scores, MASKED)
        highest = jnp.max(scores, axis=1, keepdims=True)
        weights = jnp.where(in_cache, jnp.exp(scores - highest), 0.0)
        totals.append(jnp.sum(weights, axis=1, keepdims=True))
        softened.append(weights.astype(BF16))
    for copy in value_copies:
        copy.wait()
    for m in range(micro):
        weighted = jnp.dot(softened[m], values[slots[0, m]], preferred_element_type=F32)
        attended = weighted / totals[m]
        for piece in range(pieces):
            part = attended[:, piece * LANES : (piece + 1) * LANES].reshape(blocks, group, LANES).astype(BF16)
            for copy in range(copies):
                out_ref[copy, :, m, piece * group : (piece + 1) * group, :] = part


def attend(queries, key_cache, value_cache, slots, lengths, z_count, ffn_count):
    slot_count, pos, head_dim = key_cache.shape
    micro, width = queries.shape
    tile_rows = width // ffn_count // LANES
    return pl.pallas_call(
        attention_kernel,
        in_specs=[in_hbm()] * 5,
        out_specs=whole(),
        out_shape=jax.ShapeDtypeStruct((z_count, ffn_count, micro, tile_rows, LANES), BF16),
        scratch_shapes=[
            pltpu.SMEM(slots.shape, jnp.int32),
            pltpu.SMEM(lengths.shape, jnp.int32),
            pltpu.VMEM(queries.shape, BF16),
            pltpu.VMEM((slot_count, pos, head_dim), BF16),
            pltpu.VMEM((slot_count, pos, head_dim), BF16),
            pltpu.VMEM((micro, width // head_dim, head_dim), F32),
            pltpu.SemaphoreType.DMA((3,)),
            pltpu.SemaphoreType.DMA((slot_count,)),
            pltpu.SemaphoreType.DMA((slot_count,)),
        ],
        compiler_params=params(60),
        name="attention",
    )(slots, lengths, queries, key_cache, value_cache)


def spread_shares(order, own, other, source):
    z_count, _, ffn_count, micro = order
    count = own.shape[0]

    def place_of(r):
        m = r % micro
        z = (r // micro) % z_count
        share = (r // (micro * z_count)) % 2
        f = r // (micro * z_count * 2)
        return share * count + source(z, f, m)

    spread = one_hot((2 * count, 2 * count), place_of).astype(BF16)
    return jnp.dot(spread, jnp.concatenate([own, other], axis=0), preferred_element_type=F32).astype(BF16)


def rows_kernel(pieces, in_ref, out_ref, wide):
    rows, tile_rows, lanes = in_ref.shape
    wide[...] = in_ref[...].astype(F32).reshape(rows * tile_rows, lanes)
    group = tile_rows // pieces
    for j in range(tile_rows):
        at = (j % pieces) * group + j // pieces
        out_ref[:, j * lanes : (j + 1) * lanes] = wide[pl.ds(at, rows, stride=tile_rows), :].astype(BF16)


def to_rows(tiles, pieces):
    rows, tile_rows, lanes = tiles.shape
    return pl.pallas_call(
        functools.partial(rows_kernel, pieces),
        out_shape=jax.ShapeDtypeStruct((rows, tile_rows * lanes), BF16),
        in_specs=[whole()],
        out_specs=whole(),
        scratch_shapes=[pltpu.VMEM((rows * tile_rows, lanes), F32)],
        compiler_params=params(8),
        name="to_rows",
    )(tiles)


def product_kernel(rows_ref, weight_ref, out_ref):
    out_ref[...] = jnp.dot(rows_ref[...], weight_ref[...], preferred_element_type=F32).astype(BF16)


def product_of(rows, weight):
    return pl.pallas_call(
        product_kernel,
        out_shape=jax.ShapeDtypeStruct((rows.shape[0], weight.shape[1]), BF16),
        in_specs=[whole(), whole()],
        out_specs=whole(),
        compiler_params=params(12),
        cost_estimate=HEAVY,
        name="product",
    )(rows, weight)


def mix_kernel(order, core_ref, own_ref, rows_ref, weight_ref, out_ref):
    z_count, core_count, ffn_count, micro = order
    total = 2 * rows_ref.shape[0]
    product = jnp.dot(rows_ref[...], weight_ref[...], preferred_element_type=F32).astype(BF16)
    core = core_ref[0]

    def source(r):
        m = r % micro
        c = (r // micro) % core_count
        z = (r // (micro * core_count)) % z_count
        f = r // (micro * core_count * z_count)
        return (((c ^ core) * z_count + z) * ffn_count + f) * micro + m

    spread = one_hot((total, total), source).astype(BF16)
    both = jnp.concatenate([own_ref[...], product], axis=0)
    out_ref[...] = jnp.dot(spread, both, preferred_element_type=F32).astype(BF16)


def mix(core, own, rows, weight, order):
    return pl.pallas_call(
        functools.partial(mix_kernel, order),
        out_shape=jax.ShapeDtypeStruct((2 * rows.shape[0], weight.shape[1]), BF16),
        in_specs=[scalars(), whole(), whole(), whole()],
        out_specs=whole(),
        compiler_params=params(12),
        name="mix",
    )(core, own, rows, weight)


def down_most_kernel(*refs):
    *piece_refs, own_ref, other_ref, own_out_ref, other_out_ref = refs
    rows = jnp.concatenate([ref[...] for ref in piece_refs], axis=0)
    own_out_ref[...] = jnp.dot(rows, own_ref[...], preferred_element_type=F32).astype(BF16)
    other_out_ref[...] = jnp.dot(rows, other_ref[...], preferred_element_type=F32).astype(BF16)


def down_most(pieces, own_weight, other_weight):
    shape = jax.ShapeDtypeStruct((len(pieces) * pieces[0].shape[0], own_weight.shape[1]), BF16)
    return pl.pallas_call(
        down_most_kernel,
        out_shape=(shape, shape),
        in_specs=[whole()] * (len(pieces) + 2),
        out_specs=(whole(), whole()),
        compiler_params=params(16),
        cost_estimate=HEAVY,
        name="down_most",
    )(*pieces, own_weight, other_weight)


def down_kernel(order, z_ref, own_most_ref, other_most_ref, rows_ref, own_ref, other_ref, out_ref):
    _, _, ffn_count, micro = order
    shares = []
    for most_ref, weight_ref in ((own_most_ref, own_ref), (other_most_ref, other_ref)):
        last = jnp.dot(rows_ref[...], weight_ref[...], preferred_element_type=F32).astype(BF16)
        shares.append(jnp.concatenate([most_ref[...], last], axis=0))
    me = z_ref[0]
    out_ref[...] = spread_shares(order, *shares, lambda z, f, m: ((z ^ me) * ffn_count + f) * micro + m)


def down(z, most, last, own_weight, other_weight, order):
    rows = most[0].shape[0] + last.shape[0]
    return pl.pallas_call(
        functools.partial(down_kernel, order),
        out_shape=jax.ShapeDtypeStruct((2 * rows, own_weight.shape[1]), BF16),
        in_specs=[scalars()] + [whole()] * 5,
        out_specs=whole(),
        compiler_params=params(16),
        name="down",
    )(z, *most, last, own_weight, other_weight)


def fetch_kernel(cuts, *refs):
    count = (len(refs) - 1) // 2
    sources, targets, sems = refs[:count], refs[count : 2 * count], refs[2 * count]
    copies = []
    for i in range(count):
        rows = sources[i].shape[0] // cuts
        for j in range(cuts):
            part = pl.ds(j * rows, rows)
            copies.append(pltpu.make_async_copy(sources[i].at[part], targets[i].at[part], sems.at[i * cuts + j]))
    for copy in copies:
        copy.start()
    for copy in copies:
        copy.wait()


def fetch(*arrays):
    cuts = 4
    return pl.pallas_call(
        functools.partial(fetch_kernel, cuts),
        out_shape=[jax.ShapeDtypeStruct(array.shape, array.dtype) for array in arrays],
        in_specs=[in_hbm()] * len(arrays),
        out_specs=[whole()] * len(arrays),
        scratch_shapes=[pltpu.SemaphoreType.DMA((len(arrays) * cuts,))],
        compiler_params=params(16),
        cost_estimate=HEAVY,
        name="fetch",
    )(*arrays)


def sum_parts(parts_ref):
    total = parts_ref[0].astype(F32)
    for j in range(1, parts_ref.shape[0]):
        total = total + parts_ref[j].astype(F32)
    return total


def stream_kernel(order, f_ref, core_ref, parts_ref, hidden_ref, stream_ref, send_ref, copies_ref):
    z_count, core_count, ffn_count, micro = order
    rows = stream_ref.shape[0]
    f = f_ref[0]

    def source(r):
        return ((r % micro) * z_count * core_count + r // micro) * ffn_count + f

    spread = one_hot((rows, hidden_ref.shape[0]), source).astype(BF16)
    hidden = jnp.dot(spread, hidden_ref[...], preferred_element_type=F32)
    stream = (hidden + sum_parts(parts_ref)).astype(BF16)
    stream_ref[...] = stream
    for j in range(copies_ref.shape[0]):
        copies_ref[j] = stream

    def other(r):
        row = ((r // micro) * core_count + 1 - core_ref[0]) * micro + r % micro
        return jnp.where(r < z_count * micro, row, -1)

    pick = one_hot((FEW, rows), other).astype(BF16)
    send_ref[...] = jnp.dot(pick, stream, preferred_element_type=F32).astype(BF16)


def make_stream(f, core, parts, hidden, order):
    _, rows, width = parts.shape
    return pl.pallas_call(
        functools.partial(stream_kernel, order),
        out_shape=(
            jax.ShapeDtypeStruct((rows, width), BF16),
            jax.ShapeDtypeStruct((FEW, width), BF16),
            jax.ShapeDtypeStruct(parts.shape, BF16),
        ),
        in_specs=[scalars()] * 2 + [whole()] * 2,
        out_specs=(whole(), whole(), whole()),
        compiler_params=params(8),
        name="make_stream",
    )(f, core, parts, hidden)


def squares_rows(row_values, width):
    high = row_values.astype(BF16).astype(F32)
    low = row_values - high
    index = lax.broadcasted_iota(jnp.int32, (SQ_ROWS, width), 0)
    return jnp.where(index == 0, high, jnp.where(index == 1, low, 0.0)).astype(BF16)


def up_kernel(order, hops, z_ref, core_ref, stream_ref, gain_ref, gate_ref, up_ref, *out_refs):
    z_count, core_count, ffn_count, micro = order
    tiles = gate_ref.shape[1] // LANES
    rows = ffn_count * micro
    me = z_ref[0]
    core = core_ref[0]

    def source(r):
        m = r % micro
        f = (r // micro) % ffn_count
        block = r // rows
        side = block // len(hops)
        hop = hops[0] + block % len(hops)
        return ((f * z_count + (me ^ hop)) * core_count + (core ^ side)) * micro + m

    spread = one_hot((len(out_refs) * rows, stream_ref.shape[0]), source).astype(BF16)
    stream = jnp.dot(spread, stream_ref[...], preferred_element_type=F32)
    scaled = (stream * gain_ref[...].astype(F32)).astype(BF16)
    squares = jnp.sum(stream * stream, axis=1, keepdims=True)
    lane = one_hot((rows, LANES), lambda r: r)
    for i, out_ref in enumerate(out_refs):
        sums = jnp.sum(lane * squares[i * rows : (i + 1) * rows], axis=0, keepdims=True)
        out_ref[2 * tiles * rows :, :] = squares_rows(sums, LANES)
    for half, weight_ref in enumerate((gate_ref, up_ref)):
        product = jnp.dot(scaled, weight_ref[...], preferred_element_type=F32).astype(BF16)
        for i, out_ref in enumerate(out_refs):
            for j in range(tiles):
                at = (half * tiles + j) * rows
                out_ref[at : at + rows, :] = product[i * rows : (i + 1) * rows, j * LANES : (j + 1) * LANES]


def up_part(order, hops, z, core, stream_all, gain, gate_weight, up_weight):
    _, _, ffn_count, micro = order
    out_rows = 2 * gate_weight.shape[1] // LANES * ffn_count * micro + SQ_ROWS
    shape = jax.ShapeDtypeStruct((out_rows, LANES), BF16)
    return pl.pallas_call(
        functools.partial(up_kernel, order, hops),
        out_shape=[shape] * (2 * len(hops)),
        in_specs=[scalars(), scalars(), whole(), whole(), whole(), whole()],
        out_specs=[whole()] * (2 * len(hops)),
        compiler_params=params(16),
        cost_estimate=HEAVY,
        name="up_part",
    )(z, core, stream_all, gain, gate_weight, up_weight)


def sum_blocks(refs, start, stop):
    total = refs[0][start:stop, :].astype(F32)
    for ref in refs[1:]:
        total = total + ref[start:stop, :].astype(F32)
    return total


def add_kernel(*refs):
    *block_refs, out_ref = refs
    out_rows, lanes = out_ref.shape
    body = out_rows - SQ_ROWS
    out_ref[:body, :] = sum_blocks(block_refs, 0, body).astype(BF16)
    tail = sum_blocks(block_refs, body, out_rows)
    out_ref[body:, :] = squares_rows(tail[0:1] + tail[1:2], lanes)


def add(*blocks):
    return pl.pallas_call(
        add_kernel,
        out_shape=jax.ShapeDtypeStruct(blocks[0].shape, BF16),
        in_specs=[whole()] * len(blocks),
        out_specs=whole(),
        compiler_params=params(8),
        name="add",
    )(*blocks)


def activate_kernel(model_width, *refs):
    *block_refs, out_ref = refs
    out_rows, lanes = block_refs[0].shape
    rows, hidden = out_ref.shape
    tiles = hidden // lanes
    tail = sum_blocks(block_refs, out_rows - SQ_ROWS, out_rows)
    lane_sums = tail[0:1] + tail[1:2]
    spread = one_hot((rows, lanes), lambda r: r)
    squares = jnp.sum(spread * lane_sums, axis=1, keepdims=True)
    scale = lax.rsqrt(squares / model_width + EPSILON)
    for j in range(tiles):
        gate = sum_blocks(block_refs, j * rows, (j + 1) * rows) * scale
        upward = sum_blocks(block_refs, (tiles + j) * rows, (tiles + j + 1) * rows) * scale
        out_ref[:, j * lanes : (j + 1) * lanes] = (gate / (1.0 + jnp.exp(-gate)) * upward).astype(BF16)


def activate(blocks, rows, hidden, model_width):
    return pl.pallas_call(
        functools.partial(activate_kernel, model_width),
        out_shape=jax.ShapeDtypeStruct((rows, hidden), BF16),
        in_specs=[whole()] * len(blocks),
        out_specs=whole(),
        compiler_params=params(8),
        name="activate",
    )(*blocks)


def finish_kernel(order, z_ref, core_ref, parts_ref, stream_ref, received_ref, *out_refs):
    z_count, core_count, _, micro = order
    rows = stream_ref.shape[0]
    half = rows // 2

    def own(r):
        return jnp.where(r < half, ((r // micro) * core_count + core_ref[0]) * micro + r % micro, -1)

    first = one_hot((rows, rows), own).astype(BF16)
    second = one_hot((rows, FEW), lambda r: r - half).astype(BF16)
    stream = jnp.dot(first, stream_ref[...], preferred_element_type=F32)
    stream = stream + jnp.dot(second, received_ref[...], preferred_element_type=F32)
    finished = (stream + sum_parts(parts_ref)).astype(BF16)
    slots = out_refs[0].shape[0]
    me = z_ref[0]

    def source(r):
        q = r % slots
        at = (q // micro) * half + ((r // slots) ^ me) * micro + q % micro
        return jnp.where(q < 2 * micro, at, -1)

    spread = one_hot((len(out_refs) * slots, rows), source).astype(BF16)
    blocks = jnp.dot(spread, finished, preferred_element_type=F32)
    for k, out_ref in enumerate(out_refs):
        out_ref[...] = blocks[k * slots : (k + 1) * slots].astype(BF16)


def finish(z, core, parts, stream, received, order):
    z_count, _, _, micro = order
    slots = -(-2 * micro // 8) * 8
    return pl.pallas_call(
        functools.partial(finish_kernel, order),
        out_shape=[jax.ShapeDtypeStruct((slots, stream.shape[1]), BF16)] * z_count,
        in_specs=[scalars()] * 2 + [whole()] * 3,
        out_specs=[whole()] * z_count,
        compiler_params=params(8),
        name="finish",
    )(z, core, parts, stream, received)


def place_kernel(z_ref, core_ref, *refs):
    *piece_refs, out_ref = refs
    width = piece_refs[0].shape[1]
    micro = out_ref.shape[0]
    for k, ref in enumerate(piece_refs):
        block = ref[...].astype(F32)
        for side in range(2):
            share = 2 * (z_ref[0] ^ k) + (core_ref[0] ^ side)
            at = pl.multiple_of(share * width, LANES)
            out_ref[:, pl.ds(at, width)] = block[side * micro : (side + 1) * micro].astype(BF16)


def place(z, core, pieces, micro):
    width = pieces[0].shape[1]
    return pl.pallas_call(
        place_kernel,
        out_shape=jax.ShapeDtypeStruct((micro, 2 * len(pieces) * width), BF16),
        in_specs=[scalars(), scalars()] + [whole()] * len(pieces),
        out_specs=whole(),
        compiler_params=params(8),
        name="place",
    )(z, core, *pieces)


def along_z(array, hop):
    return lax.ppermute(array, Z, [(i, i ^ hop) for i in range(lax.axis_size(Z))])


def swap_cores(array):
    return lax.ppermute(array, CORE, [(0, 1), (1, 0)])


def per_device(
    hidden_in,
    queries,
    key_cache,
    value_cache,
    lengths,
    cache_slot,
    out_weight,
    ffn_gain,
    gate_weight,
    up_weight,
    down_weight,
):
    z_count = lax.axis_size(Z)
    core_count = lax.axis_size(CORE)
    attn_count = z_count * core_count
    ffn_count = lax.axis_size("x") * lax.axis_size("y")
    f_index = lax.axis_index(FFN).astype(jnp.int32)[None]
    z_index = lax.axis_index(Z).astype(jnp.int32)[None]
    core_index = lax.axis_index(CORE).astype(jnp.int32)[None]
    micro, total_rows, col_share = hidden_in.shape
    head_dim = key_cache.shape[2]
    model_width = col_share * attn_count
    hidden_share = gate_weight.shape[1]
    rows_chunk = attn_count * micro
    rows_all = ffn_count * rows_chunk
    rows_block = rows_all // attn_count

    order = (z_count, core_count, ffn_count, micro)
    payload = attend(
        queries.reshape(micro, -1), key_cache, value_cache, cache_slot.T, lengths.T, z_count, ffn_count
    )
    tile_rows = payload.shape[3]
    payload, f_index, z_index, core_index = lax.optimization_barrier((payload, f_index, z_index, core_index))
    payload = payload.reshape(z_count * ffn_count, micro * tile_rows, LANES)
    incoming = lax.all_to_all(payload, (Z,) + FFN, split_axis=0, concat_axis=0, tiled=True)
    own_rows = to_rows(incoming.reshape(z_count * ffn_count * micro, tile_rows, LANES), head_dim // LANES)
    own_rows, ffn_gain = lax.optimization_barrier((own_rows, ffn_gain))
    other_rows = swap_cores(own_rows)
    gain = ffn_gain[None, :]
    own_mixed = product_of(own_rows, out_weight)
    own_mixed, other_rows, gain = lax.optimization_barrier((own_mixed, other_rows, gain))
    mixed = mix(core_index, own_mixed, other_rows, out_weight, order)

    parts = lax.all_to_all(
        mixed.reshape(ffn_count, rows_chunk, col_share), FFN, split_axis=0, concat_axis=0, tiled=True
    )
    stream, send, copies = make_stream(f_index, core_index, parts, hidden_in.reshape(rows_all, col_share), order)
    stream_all = lax.all_to_all(copies, FFN, split_axis=0, concat_axis=0, tiled=True)
    stream_all = stream_all.reshape(rows_all, col_share)

    up_args = (gain, gate_weight, up_weight)
    own2, own3, other2, other3 = up_part(order, (2, 3), z_index, core_index, stream_all, *up_args)
    own0, own1, other0, other1 = up_part(order, (0, 1), z_index, core_index, stream_all, *up_args)
    received3, own0 = lax.optimization_barrier((swap_cores(other3), own0))
    relayed3 = add(own3, received3)
    relayed3, other0, other1, other2 = lax.optimization_barrier((relayed3, other0, other1, other2))
    crossing = along_z(relayed3, 1)
    near1 = add(own1, swap_cores(other1))
    received2, near1 = lax.optimization_barrier((swap_cores(other2), near1))
    relayed = add(own2, received2, crossing)
    relayed, send = lax.optimization_barrier((relayed, send))
    from_far = along_z(relayed, 2)
    from_near = along_z(near1, 1)
    down_weight, near1 = lax.optimization_barrier((down_weight, near1))
    down_own, down_other = fetch(down_weight, swap_cores(down_weight))
    from_far, down_own, down_other = lax.optimization_barrier((from_far, down_own, down_other))
    activated = activate((own0, swap_cores(other0), from_near, from_far), rows_block, hidden_share, model_width)

    far = along_z(activated, 2)
    near = along_z(activated, 1)
    far, received = lax.optimization_barrier((far, swap_cores(send)))
    most = down_most((activated, near, far), down_own, down_other)
    lowered = down(z_index, most, along_z(far, 1), down_own, down_other, order)
    lowered_parts = lax.all_to_all(
        lowered.reshape(ffn_count, rows_chunk, col_share), FFN, split_axis=0, concat_axis=0, tiled=True
    )
    shares = finish(z_index, core_index, lowered_parts, stream, received, order)
    pieces = [shares[0]] + [along_z(shares[hop], hop) for hop in range(1, z_count)]
    return place(z_index, core_index, pieces, micro).reshape(micro, 1, model_width)


def solution(mesh):
    sizes = dict(mesh.shape)
    attn_count, ffn_count, rep_count = sizes["attn"], sizes["ffn"], sizes["rep"]
    side = int(round(ffn_count**0.5))
    fine = Mesh(
        mesh.devices.reshape(attn_count // 2, 2, side, ffn_count // side, rep_count),
        (Z, CORE, "x", "y", REP),
    )
    owners = (REP, Z, CORE, "x", "y")
    return jax.shard_map(
        per_device,
        mesh=fine,
        in_specs=(
            P(None, REP, ATTN),
            P(None, owners, None),
            P(owners, None, None),
            P(owners, None, None),
            P(None, owners),
            P(None, owners),
            P(FFN, ATTN),
            P(ATTN),
            P(ATTN, FFN),
            P(ATTN, FFN),
            P(FFN, ATTN),
        ),
        out_specs=P(None, owners, None),
        check_vma=False,
    )
```

profile of v0, /device:TPU:8, one launch (start us, length us, event | category | flops | bytes accessed | tf_op | source)
XLA Modules:
  0.0 128.0 jit_solution(17210215964366618104)
XLA Ops:
  0.0 4.0 %attention.1 = bf16[4,16,3,8,128]{4,3,2,1,0:T(8,128)(2,1)} custom-call(s32[1,3]{1,0:T(1,128)} %bitcast.21, s32[1,3]{1,0:T(1,128)} %bitcast.22, bf16[3,16384]{1,0:T(4,128)(2,1)} %bitcast.20, bf16[3,1024,256]{2,1,0:T(8,128)(2,1)} %key_hbm.1, bf16[3,1024,256]{2,1,0:T(8,128)(2,1)} %value_hbm.1), custom_call_target="tpu_custom_call" | custom-call | tf_op jit(solution)/shard_map/attention/pallas_call | solution.py:112
  4.0 26.3 %all_to_all.20 = bf16[64,24,128]{2,1,0:T(8,128)(2,1)S(1)} all-to-all(bf16[64,24,128]{2,1,0:T(8,128)(2,1)} %bitcast.19), channel_id=1, replica_groups=mesh['z'=4,'core'=2,'x'=4,'y'=4,'rep'=2] {'z','x','y'}, dimensions={0} | all-to-all | bytes 786432 | tf_op jit(solution)/shard_map/all_to_all | solution.py:546
  31.3 1.1 collective-permute-done.rows_ref
  32.4 1.1 mix.1
  33.5 16.8 %all_to_all.21.parts_ref = bf16[16,24,896]{2,1,0:T(8,128)(2,1)S(1)} all-to-all(bf16[16,24,896]{2,1,0:T(8,128)(2,1)S(1)} %bitcast.14), channel_id=1, replica_groups=mesh['z'=4,'core'=2,'x'=4,'y'=4,'rep'=2] {'x','y'}, dimensions={0} | all-to-all | bytes 1376256 | tf_op jit(solution)/shard_map/all_to_all | solution.py:555
  50.6 15.6 %all_to_all.22 = bf16[16,24,896]{2,1,0:T(8,128)(2,1)S(1)} all-to-all(bf16[16,24,896]{2,1,0:T(8,128)(2,1)S(1)} %get-tuple-element.57), channel_id=1, replica_groups=mesh['z'=4,'core'=2,'x'=4,'y'=4,'rep'=2] {'x','y'}, dimensions={0} | all-to-all | bytes 1376256 | tf_op jit(solution)/shard_map/all_to_all | solution.py:559
  66.3 1.5 %up_part.2 = (bf16[880,128]{1,0:T(8,128)(2,1)S(1)}, bf16[880,128]{1,0:T(8,128)(2,1)S(1)}, bf16[880,128]{1,0:T(8,128)(2,1)S(1)}, bf16[880,128]{1,0:T(8,128)(2,1)S(1)}) custom-call(s32[1]{0:T(128)} %bitcast.4.z_ref, s32[1]{0:T(128)} %bitcast.5.core_ref, bf16[384,896]{1,0:T(8,128)(2,1)S(1)} %bitcast.17, bf16[1,896]{1,0:T(2,128)(2,1)S(1)} %broadcast_in_dim.15.gain_ref, ...), custom_call_target="tpu_custom_call" | custom-call | flops 10000000000 | bytes 10000000 | tf_op jit(solution)/shard_map/up_part/pallas_call | solution.py:374
  67.9 1.5 %up_part.3 = (bf16[880,128]{1,0:T(8,128)(2,1)S(1)}, bf16[880,128]{1,0:T(8,128)(2,1)S(1)}, bf16[880,128]{1,0:T(8,128)(2,1)S(1)}, bf16[880,128]{1,0:T(8,128)(2,1)S(1)}) custom-call(s32[1]{0:T(128)} %bitcast.4.z_ref, s32[1]{0:T(128)} %bitcast.5.core_ref, bf16[384,896]{1,0:T(8,128)(2,1)S(1)} %bitcast.18, bf16[1,896]{1,0:T(2,128)(2,1)S(1)} %broadcast_in_dim.15.gain_ref, ...), custom_call_target="tpu_custom_call" | custom-call | flops 10000000000 | bytes 10000000 | tf_op jit(solution)/shard_map/up_part/pallas_call | solution.py:374
  70.2 1.0 collective-permute-done.4.refs_1_
  72.4 1.4 %collective-permute-start.5 = (bf16[880,128]{1,0:T(8,128)(2,1)S(1)}, bf16[880,128]{1,0:T(8,128)(2,1)S(1)}, u32[]{:S(2)}, u32[]{:S(2)}) collective-permute-start(bf16[880,128]{1,0:T(8,128)(2,1)S(1)} %add.8), channel_id=1, source_target_pairs={{0,64},{64,0},{128,192},{192,128},{1,65},{65,1},{129,193},{193,129... | collective-permute-start | bytes 675848 | tf_op jit(solution)/shard_map/ppermute | solution.py:504
  73.9 6.3 %collective-permute-done.6.refs_2_ = bf16[880,128]{1,0:T(8,128)(2,1)S(1)} collective-permute-done((bf16[880,128]{1,0:T(8,128)(2,1)S(1)}, bf16[880,128]{1,0:T(8,128)(2,1)S(1)}, u32[]{:S(2)}, u32[]{:S(2)}) %collective-permute-start.6) | collective-permute-done | bytes 225312 | tf_op jit(solution)/shard_map/ppermute | solution.py:504
  80.3 1.1 collective-permute-start.7
  81.4 2.8 %fetch.1 = (bf16[1152,896]{1,0:T(8,128)(2,1)S(1)}, bf16[1152,896]{1,0:T(8,128)(2,1)S(1)}) custom-call(bf16[1152,896]{1,0:T(8,128)(2,1)S(1)} %copy-done.4, bf16[1152,896]{1,0:T(8,128)(2,1)S(1)} %collective-permute-done.8.refs_1_), custom_call_target="tpu_custom_call" | custom-call | flops 10000000000 | bytes 10000000 | tf_op jit(solution)/shard_map/fetch/pallas_call | solution.py:274
  84.3 8.1 %collective-permute-done.7.refs_3_ = bf16[880,128]{1,0:T(8,128)(2,1)S(1)} collective-permute-done((bf16[880,128]{1,0:T(8,128)(2,1)S(1)}, bf16[880,128]{1,0:T(8,128)(2,1)S(1)}, u32[]{:S(2)}, u32[]{:S(2)}) %collective-permute-start.7) | collective-permute-done | bytes 225312 | tf_op jit(solution)/shard_map/ppermute | solution.py:504
  92.7 2.3 %collective-permute-start.9 = (bf16[48,1152]{1,0:T(8,128)(2,1)S(1)}, bf16[48,1152]{1,0:T(8,128)(2,1)S(1)}, u32[]{:S(2)}, u32[]{:S(2)}) collective-permute-start(bf16[48,1152]{1,0:T(8,128)(2,1)S(1)} %activate.1.refs_0_), channel_id=1, source_target_pairs={{0,64},{64,0},{128,192},{192,128},{1,65},{65,1},{129,193},{193,129... | collective-permute-start | bytes 331784 | tf_op jit(solution)/shard_map/ppermute | solution.py:504
  95.1 1.2 collective-permute-done.11.received_ref
  96.3 2.7 %collective-permute-done.10.refs_2_ = bf16[48,1152]{1,0:T(8,128)(2,1)S(1)} collective-permute-done((bf16[48,1152]{1,0:T(8,128)(2,1)S(1)}, bf16[48,1152]{1,0:T(8,128)(2,1)S(1)}, u32[]{:S(2)}, u32[]{:S(2)}) %collective-permute-start.10) | collective-permute-done | bytes 110624 | tf_op jit(solution)/shard_map/ppermute | solution.py:504
  99.0 0.9 down_most.1
  99.9 3.8 %collective-permute-done.12.rows_ref = bf16[48,1152]{1,0:T(8,128)(2,1)S(1)} collective-permute-done((bf16[48,1152]{1,0:T(8,128)(2,1)S(1)}, bf16[48,1152]{1,0:T(8,128)(2,1)S(1)}, u32[]{:S(2)}, u32[]{:S(2)}) %collective-permute-start.12) | collective-permute-done | bytes 110624 | tf_op jit(solution)/shard_map/ppermute | solution.py:504
  103.7 1.3 %down.1 = bf16[384,896]{1,0:T(8,128)(2,1)S(1)} custom-call(s32[1]{0:T(128)} %bitcast.4.z_ref, bf16[144,896]{1,0:T(8,128)(2,1)S(1)} %get-tuple-element.85.own_most_ref, bf16[144,896]{1,0:T(8,128)(2,1)S(1)} %get-tuple-element.86.other_most_ref, bf16[48,1152]{1,0:T(8,128)(2,1)S(1)} %collective-permute-done.12.rows_ref, ...), custom_call_target="tpu_custom_call" | custom-call | tf_op jit(solution)/shard_map/down/pallas_call | solution.py:247
  105.0 14.2 %all_to_all.23.parts_ref = bf16[16,24,896]{2,1,0:T(8,128)(2,1)S(1)} all-to-all(bf16[16,24,896]{2,1,0:T(8,128)(2,1)S(1)} %bitcast.13), channel_id=1, replica_groups=mesh['z'=4,'core'=2,'x'=4,'y'=4,'rep'=2] {'x','y'}, dimensions={0} | all-to-all | bytes 1376256 | tf_op jit(solution)/shard_map/all_to_all | solution.py:585
  119.7 2.1 %collective-permute-start.14 = (bf16[8,896]{1,0:T(8,128)(2,1)S(1)}, bf16[8,896]{1,0:T(8,128)(2,1)S(1)}, u32[]{:S(2)}, u32[]{:S(2)}) collective-permute-start(bf16[8,896]{1,0:T(8,128)(2,1)S(1)} %get-tuple-element.91), channel_id=1, source_target_pairs={{0,128},{64,192},{128,0},{192,64},{1,129},{65,193},{129,1},{193,65... | collective-permute-start | bytes 43016 | tf_op jit(solution)/shard_map/ppermute | solution.py:504
  121.8 2.2 %collective-permute-start.15 = (bf16[8,896]{1,0:T(8,128)(2,1)S(1)}, bf16[8,896]{1,0:T(8,128)(2,1)S(1)}, u32[]{:S(2)}, u32[]{:S(2)}) collective-permute-start(bf16[8,896]{1,0:T(8,128)(2,1)S(1)} %get-tuple-element.92), channel_id=1, source_target_pairs={{0,192},{64,128},{128,64},{192,0},{1,193},{65,129},{129,65},{193,1... | collective-permute-start | bytes 43016 | tf_op jit(solution)/shard_map/ppermute | solution.py:504
  124.3 3.0 %collective-permute-done.15.refs_3_ = bf16[8,896]{1,0:T(8,128)(2,1)S(1)} collective-permute-done((bf16[8,896]{1,0:T(8,128)(2,1)S(1)}, bf16[8,896]{1,0:T(8,128)(2,1)S(1)}, u32[]{:S(2)}, u32[]{:S(2)}) %collective-permute-start.15) | collective-permute-done | bytes 14368 | tf_op jit(solution)/shard_map/ppermute | solution.py:504
  (41 shorter events, 5.2 us)
Async XLA Ops:
  0.0 30.6 %copy-start = (bf16[1024,896]{1,0:T(8,128)(2,1)S(1)}, bf16[1024,896]{1,0:T(8,128)(2,1)}, u32[]{:S(2)}) copy-start(bf16[1024,896]{1,0:T(8,128)(2,1)} %weight_ref.3) | copy-start | bytes 5505028
  30.5 0.7 copy-start.5
  30.5 1.8 %collective-permute-start = (bf16[192,1024]{1,0:T(8,128)(2,1)S(1)}, bf16[192,1024]{1,0:T(8,128)(2,1)S(1)}, u32[]{:S(2)}, u32[]{:S(2)}) collective-permute-start(bf16[192,1024]{1,0:T(8,128)(2,1)S(1)} %to_rows.1.rows_ref), channel_id=1, source_target_pairs={{0,32},{32,0},{1,33},{33,1},{2,34},{34,2},{3,35},{35,3},{4,36},{36... | collective-permute-start | bytes 1179656 | tf_op jit(solution)/shard_map/ppermute | solution.py:508
  31.3 19.0 %copy-start.1 = (bf16[3,128,896]{2,1,0:T(8,128)(2,1)S(1)}, bf16[3,128,896]{2,1,0:T(8,128)(2,1)}, u32[]{:S(2)}) copy-start(bf16[3,128,896]{2,1,0:T(8,128)(2,1)} %param.11) | copy-start | bytes 2064388
  33.5 32.8 %copy-start.2 = (bf16[896,1152]{1,0:T(8,128)(2,1)S(1)}, bf16[896,1152]{1,0:T(8,128)(2,1)}, u32[]{:S(2)}) copy-start(bf16[896,1152]{1,0:T(8,128)(2,1)} %gate_ref.3) | copy-start | bytes 6193156
  33.5 32.8 %copy-start.3 = (bf16[896,1152]{1,0:T(8,128)(2,1)S(1)}, bf16[896,1152]{1,0:T(8,128)(2,1)}, u32[]{:S(2)}) copy-start(bf16[896,1152]{1,0:T(8,128)(2,1)} %up_ref.3) | copy-start | bytes 6193156
  67.8 3.8 %copy-start.4 = (bf16[1152,896]{1,0:T(8,128)(2,1)S(1)}, bf16[1152,896]{1,0:T(8,128)(2,1)}, u32[]{:S(2)}) copy-start(bf16[1152,896]{1,0:T(8,128)(2,1)} %refs_0_) | copy-start | bytes 6193156
  67.8 1.6 %collective-permute-start.1 = (bf16[880,128]{1,0:T(8,128)(2,1)S(1)}, bf16[880,128]{1,0:T(8,128)(2,1)S(1)}, u32[]{:S(2)}, u32[]{:S(2)}) collective-permute-start(bf16[880,128]{1,0:T(8,128)(2,1)S(1)} %get-tuple-element.59), channel_id=1, source_target_pairs={{0,32},{32,0},{1,33},{33,1},{2,34},{34,2},{3,35},{35,3},{4,36},{36... | collective-permute-start | bytes 675848 | tf_op jit(solution)/shard_map/ppermute | solution.py:508
  69.5 1.7 %collective-permute-start.4 = (bf16[880,128]{1,0:T(8,128)(2,1)S(1)}, bf16[880,128]{1,0:T(8,128)(2,1)S(1)}, u32[]{:S(2)}, u32[]{:S(2)}) collective-permute-start(bf16[880,128]{1,0:T(8,128)(2,1)S(1)} %get-tuple-element.70), channel_id=1, source_target_pairs={{0,32},{32,0},{1,33},{33,1},{2,34},{34,2},{3,35},{35,3},{4,36},{36... | collective-permute-start | bytes 675848 | tf_op jit(solution)/shard_map/ppermute | solution.py:508
  70.1 1.5 %collective-permute-start.3 = (bf16[880,128]{1,0:T(8,128)(2,1)S(1)}, bf16[880,128]{1,0:T(8,128)(2,1)S(1)}, u32[]{:S(2)}, u32[]{:S(2)}) collective-permute-start(bf16[880,128]{1,0:T(8,128)(2,1)S(1)} %get-tuple-element.68), channel_id=1, source_target_pairs={{0,32},{32,0},{1,33},{33,1},{2,34},{34,2},{3,35},{35,3},{4,36},{36... | collective-permute-start | bytes 675848 | tf_op jit(solution)/shard_map/ppermute | solution.py:508
  71.5 9.9 %collective-permute-start.8 = (bf16[1152,896]{1,0:T(8,128)(2,1)S(1)}, bf16[1152,896]{1,0:T(8,128)(2,1)S(1)}, u32[]{:S(2)}, u32[]{:S(2)}) collective-permute-start(bf16[1152,896]{1,0:T(8,128)(2,1)S(1)} %copy-done.4), channel_id=1, source_target_pairs={{0,32},{32,0},{1,33},{33,1},{2,34},{34,2},{3,35},{35,3},{4,36},{36... | collective-permute-start | bytes 6193160 | tf_op jit(solution)/shard_map/ppermute | solution.py:508
  71.9 8.4 %collective-permute-start.6 = (bf16[880,128]{1,0:T(8,128)(2,1)S(1)}, bf16[880,128]{1,0:T(8,128)(2,1)S(1)}, u32[]{:S(2)}, u32[]{:S(2)}) collective-permute-start(bf16[880,128]{1,0:T(8,128)(2,1)S(1)} %add.7), channel_id=1, source_target_pairs={{0,64},{64,0},{128,192},{192,128},{1,65},{65,1},{129,193},{193,129... | collective-permute-start | bytes 675848 | tf_op jit(solution)/shard_map/ppermute | solution.py:504
  72.4 20.0 %collective-permute-start.2 = (bf16[880,128]{1,0:T(8,128)(2,1)S(1)}, bf16[880,128]{1,0:T(8,128)(2,1)S(1)}, u32[]{:S(2)}, u32[]{:S(2)}) collective-permute-start(bf16[880,128]{1,0:T(8,128)(2,1)S(1)} %get-tuple-element.67), channel_id=1, source_target_pairs={{0,32},{32,0},{1,33},{33,1},{2,34},{34,2},{3,35},{35,3},{4,36},{36... | collective-permute-start | bytes 675848 | tf_op jit(solution)/shard_map/ppermute | solution.py:508
  72.4 20.0 %collective-permute-start.5 = (bf16[880,128]{1,0:T(8,128)(2,1)S(1)}, bf16[880,128]{1,0:T(8,128)(2,1)S(1)}, u32[]{:S(2)}, u32[]{:S(2)}) collective-permute-start(bf16[880,128]{1,0:T(8,128)(2,1)S(1)} %add.8), channel_id=1, source_target_pairs={{0,64},{64,0},{128,192},{192,128},{1,65},{65,1},{129,193},{193,129... | collective-permute-start | bytes 675848 | tf_op jit(solution)/shard_map/ppermute | solution.py:504
  80.3 12.1 %collective-permute-start.7 = (bf16[880,128]{1,0:T(8,128)(2,1)S(1)}, bf16[880,128]{1,0:T(8,128)(2,1)S(1)}, u32[]{:S(2)}, u32[]{:S(2)}) collective-permute-start(bf16[880,128]{1,0:T(8,128)(2,1)S(1)} %add.9), channel_id=1, source_target_pairs={{0,128},{64,192},{128,0},{192,64},{1,129},{65,193},{129,1},{193,65... | collective-permute-start | bytes 675848 | tf_op jit(solution)/shard_map/ppermute | solution.py:504
  92.6 6.4 %collective-permute-start.10 = (bf16[48,1152]{1,0:T(8,128)(2,1)S(1)}, bf16[48,1152]{1,0:T(8,128)(2,1)S(1)}, u32[]{:S(2)}, u32[]{:S(2)}) collective-permute-start(bf16[48,1152]{1,0:T(8,128)(2,1)S(1)} %activate.1.refs_0_), channel_id=1, source_target_pairs={{0,128},{64,192},{128,0},{192,64},{1,129},{65,193},{129,1},{193,65... | collective-permute-start | bytes 331784 | tf_op jit(solution)/shard_map/ppermute | solution.py:504
  92.7 6.3 %collective-permute-start.9 = (bf16[48,1152]{1,0:T(8,128)(2,1)S(1)}, bf16[48,1152]{1,0:T(8,128)(2,1)S(1)}, u32[]{:S(2)}, u32[]{:S(2)}) collective-permute-start(bf16[48,1152]{1,0:T(8,128)(2,1)S(1)} %activate.1.refs_0_), channel_id=1, source_target_pairs={{0,64},{64,0},{128,192},{192,128},{1,65},{65,1},{129,193},{193,129... | collective-permute-start | bytes 331784 | tf_op jit(solution)/shard_map/ppermute | solution.py:504
  95.1 1.2 collective-permute-start.11
  99.0 4.7 %collective-permute-start.12 = (bf16[48,1152]{1,0:T(8,128)(2,1)S(1)}, bf16[48,1152]{1,0:T(8,128)(2,1)S(1)}, u32[]{:S(2)}, u32[]{:S(2)}) collective-permute-start(bf16[48,1152]{1,0:T(8,128)(2,1)S(1)} %collective-permute-done.10.refs_2_), channel_id=1, source_target_pairs={{0,64},{64,0},{128,192},{192,128},{1,65},{65,1},{129,193},{193,129... | collective-permute-start | bytes 331784 | tf_op jit(solution)/shard_map/ppermute | solution.py:504
  119.5 4.5 %collective-permute-start.13 = (bf16[8,896]{1,0:T(8,128)(2,1)S(1)}, bf16[8,896]{1,0:T(8,128)(2,1)S(1)}, u32[]{:S(2)}, u32[]{:S(2)}) collective-permute-start(bf16[8,896]{1,0:T(8,128)(2,1)S(1)} %get-tuple-element.90), channel_id=1, source_target_pairs={{0,64},{64,0},{128,192},{192,128},{1,65},{65,1},{129,193},{193,129... | collective-permute-start | bytes 43016 | tf_op jit(solution)/shard_map/ppermute | solution.py:504
  119.7 4.7 %collective-permute-start.14 = (bf16[8,896]{1,0:T(8,128)(2,1)S(1)}, bf16[8,896]{1,0:T(8,128)(2,1)S(1)}, u32[]{:S(2)}, u32[]{:S(2)}) collective-permute-start(bf16[8,896]{1,0:T(8,128)(2,1)S(1)} %get-tuple-element.91), channel_id=1, source_target_pairs={{0,128},{64,192},{128,0},{192,64},{1,129},{65,193},{129,1},{193,65... | collective-permute-start | bytes 43016 | tf_op jit(solution)/shard_map/ppermute | solution.py:504
  121.8 5.5 %collective-permute-start.15 = (bf16[8,896]{1,0:T(8,128)(2,1)S(1)}, bf16[8,896]{1,0:T(8,128)(2,1)S(1)}, u32[]{:S(2)}, u32[]{:S(2)}) collective-permute-start(bf16[8,896]{1,0:T(8,128)(2,1)S(1)} %get-tuple-element.92), channel_id=1, source_target_pairs={{0,192},{64,128},{128,64},{192,0},{1,193},{65,129},{129,65},{193,1... | collective-permute-start | bytes 43016 | tf_op jit(solution)/shard_map/ppermute | solution.py:504
where the time goes:
time: 128 us
  blocking collectives  72.9 us (57%)
  waiting for transfers between devices  27.8 us (22%)
  Pallas kernels  15.7 us (12%)
  starting transfers between devices  11.3 us (9%)
    all_to_all x1, blocking collectives, per_device(): lax.all_to_all(payload, (Z,) + FFN, split_axis=0, concat_axis=0, tiled=True)  26.3 us
    ppermute x9, waiting for transfers between devices, along_z(): lax.ppermute(array, Z, [(i, i ^ hop) for i in range(lax.axis_size(Z))])  24.2 us
    all_to_all x1, blocking collectives, per_device(): lax.all_to_all(mixed.reshape(ffn_count, rows_chunk, col_share), FFN, spli...  16.8 us
    all_to_all x1, blocking collectives, per_device(): lax.all_to_all(copies, FFN, split_axis=0, concat_axis=0, tiled=True)  15.6 us
    all_to_all x1, blocking collectives, per_device(): lax.all_to_all(lowered.reshape(ffn_count, rows_chunk, col_share), FFN, sp...  14.2 us
    ppermute x9, starting transfers between devices, along_z(): lax.ppermute(array, Z, [(i, i ^ hop) for i in range(lax.axis_size(Z))])  10.1 us
    pallas_call x1, Pallas kernels, attend(): pl.pallas_call(attention_kernel, in_specs=[in_hbm()] * 5, out_specs=whole...  4 us
    ppermute x7, waiting for transfers between devices, swap_cores(): return lax.ppermute(array, CORE, [(0, 1), (1, 0)])  3.6 us
  transfers between devices with their start and end apart: 16, of which 10 were waited for; matrix products, arithmetic and copies ran while one was open for 0% of the time, Pallas kernels for 5%

commit v1 on v0

--- a/solution.py
+++ b/solution.py
@@ -348,7 +348,7 @@
         f = (r // micro) % ffn_count
         block = r // rows
         side = block // len(hops)
-        hop = hops[0] + block % len(hops)
+        hop = hops[0] + (hops[1] - hops[0]) * (block % len(hops))
         return ((f * z_count + (me ^ hop)) * core_count + (core ^ side)) * micro + m
 
     spread = one_hot((len(out_refs) * rows, stream_ref.shape[0]), source).astype(BF16)
@@ -559,16 +559,15 @@
     stream_all = lax.all_to_all(copies, FFN, split_axis=0, concat_axis=0, tiled=True)
     stream_all = stream_all.reshape(rows_all, col_share)
 
-    up_args = (gain, gate_weight, up_weight)
-    own2, own3, other2, other3 = up_part(order, (2, 3), z_index, core_index, stream_all, *up_args)
-    own0, own1, other0, other1 = up_part(order, (0, 1), z_index, core_index, stream_all, *up_args)
-    received3, own0 = lax.optimization_barrier((swap_cores(other3), own0))
+    up_args = (z_index, core_index, stream_all, gain, gate_weight, up_weight)
+    own3, own1, other3, other1 = up_part(order, (3, 1), *up_args)
+    own0, own2, other0, other2 = up_part(order, (0, 2), *up_args)
+    received3, received1, own0 = lax.optimization_barrier((swap_cores(other3), swap_cores(other1), own0))
     relayed3 = add(own3, received3)
-    relayed3, other0, other1, other2 = lax.optimization_barrier((relayed3, other0, other1, other2))
+    near1 = add(own1, received1)
+    relayed3, other0, other2 = lax.optimization_barrier((relayed3, other0, other2))
     crossing = along_z(relayed3, 1)
-    near1 = add(own1, swap_cores(other1))
-    received2, near1 = lax.optimization_barrier((swap_cores(other2), near1))
-    relayed = add(own2, received2, crossing)
+    relayed = add(own2, swap_cores(other2), crossing)
     relayed, send = lax.optimization_barrier((relayed, send))
     from_far = along_z(relayed, 2)
     from_near = along_z(near1, 1)

time: 128 us -> 127 us (level)
  waiting for transfers between devices: 27.8 us -> 26.3 us
    ppermute x9, waiting for transfers between devices: 24.2 us -> 22.3 us  [along_z(): lax.ppermute(array, Z, [(i, i ^ hop) for i in range(lax.axis_size(Z))])]
  transfers between devices with their start and end apart: 16 -> 16, of which waited for: 10 -> 9; matrix products, arithmetic and copies ran while one was open for 0% -> 0% of each run, Pallas kernels for 5% -> 5%
where the time goes in v1:
time: 127 us
  blocking collectives  73 us (57%)
  waiting for transfers between devices  26.3 us (21%)
  Pallas kernels  15.7 us (12%)
  starting transfers between devices  11.4 us (9%)
    all_to_all x1, blocking collectives, per_device(): lax.all_to_all(payload, (Z,) + FFN, split_axis=0, concat_axis=0, tiled=True)  26.3 us
    ppermute x9, waiting for transfers between devices, along_z(): lax.ppermute(array, Z, [(i, i ^ hop) for i in range(lax.axis_size(Z))])  22.3 us
    all_to_all x1, blocking collectives, per_device(): lax.all_to_all(mixed.reshape(ffn_count, rows_chunk, col_share), FFN, spli...  16.8 us
    all_to_all x1, blocking collectives, per_device(): lax.all_to_all(copies, FFN, split_axis=0, concat_axis=0, tiled=True)  15.6 us
    all_to_all x1, blocking collectives, per_device(): lax.all_to_all(lowered.reshape(ffn_count, rows_chunk, col_share), FFN, sp...  14.2 us
    ppermute x9, starting transfers between devices, along_z(): lax.ppermute(array, Z, [(i, i ^ hop) for i in range(lax.axis_size(Z))])  10.1 us
    ppermute x7, waiting for transfers between devices, swap_cores(): return lax.ppermute(array, CORE, [(0, 1), (1, 0)])  4.03 us
    pallas_call x1, Pallas kernels, attend(): pl.pallas_call(attention_kernel, in_specs=[in_hbm()] * 5, out_specs=whole...  4 us
  transfers between devices with their start and end apart: 16, of which 9 were waited for; matrix products, arithmetic and copies ran while one was open for 0% of the time, Pallas kernels for 5%

profile of v1, /device:TPU:8, one launch (start us, length us, event | category | flops | bytes accessed | tf_op | source)
XLA Modules:
  0.0 126.7 jit_solution(11673679837390258508)
XLA Ops:
  0.0 4.0 %attention.1 = bf16[4,16,3,8,128]{4,3,2,1,0:T(8,128)(2,1)} custom-call(s32[1,3]{1,0:T(1,128)} %bitcast.21, s32[1,3]{1,0:T(1,128)} %bitcast.22, bf16[3,16384]{1,0:T(4,128)(2,1)} %bitcast.20, bf16[3,1024,256]{2,1,0:T(8,128)(2,1)} %key_hbm.1, bf16[3,1024,256]{2,1,0:T(8,128)(2,1)} %value_hbm.1), custom_call_target="tpu_custom_call" | custom-call | tf_op jit(solution)/shard_map/attention/pallas_call | solution.py:112
  4.0 26.3 %all_to_all.20 = bf16[64,24,128]{2,1,0:T(8,128)(2,1)S(1)} all-to-all(bf16[64,24,128]{2,1,0:T(8,128)(2,1)} %bitcast.19), channel_id=1, replica_groups=mesh['z'=4,'core'=2,'x'=4,'y'=4,'rep'=2] {'z','x','y'}, dimensions={0} | all-to-all | bytes 786432 | tf_op jit(solution)/shard_map/all_to_all | solution.py:546
  31.3 1.1 collective-permute-done.rows_ref
  32.4 1.1 mix.1
  33.5 16.8 %all_to_all.21.parts_ref = bf16[16,24,896]{2,1,0:T(8,128)(2,1)S(1)} all-to-all(bf16[16,24,896]{2,1,0:T(8,128)(2,1)S(1)} %bitcast.14), channel_id=1, replica_groups=mesh['z'=4,'core'=2,'x'=4,'y'=4,'rep'=2] {'x','y'}, dimensions={0} | all-to-all | bytes 1376256 | tf_op jit(solution)/shard_map/all_to_all | solution.py:555
  50.6 15.6 %all_to_all.22 = bf16[16,24,896]{2,1,0:T(8,128)(2,1)S(1)} all-to-all(bf16[16,24,896]{2,1,0:T(8,128)(2,1)S(1)} %get-tuple-element.55), channel_id=1, replica_groups=mesh['z'=4,'core'=2,'x'=4,'y'=4,'rep'=2] {'x','y'}, dimensions={0} | all-to-all | bytes 1376256 | tf_op jit(solution)/shard_map/all_to_all | solution.py:559
  66.3 1.5 %up_part.2 = (bf16[880,128]{1,0:T(8,128)(2,1)S(1)}, bf16[880,128]{1,0:T(8,128)(2,1)S(1)}, bf16[880,128]{1,0:T(8,128)(2,1)S(1)}, bf16[880,128]{1,0:T(8,128)(2,1)S(1)}) custom-call(s32[1]{0:T(128)} %bitcast.4.z_ref, s32[1]{0:T(128)} %bitcast.5.core_ref, bf16[384,896]{1,0:T(8,128)(2,1)S(1)} %bitcast.17, bf16[1,896]{1,0:T(2,128)(2,1)S(1)} %broadcast_in_dim.15.gain_ref, ...), custom_call_target="tpu_custom_call" | custom-call | flops 10000000000 | bytes 10000000 | tf_op jit(solution)/shard_map/up_part/pallas_call | solution.py:374
  68.4 1.5 %up_part.3 = (bf16[880,128]{1,0:T(8,128)(2,1)S(1)}, bf16[880,128]{1,0:T(8,128)(2,1)S(1)}, bf16[880,128]{1,0:T(8,128)(2,1)S(1)}, bf16[880,128]{1,0:T(8,128)(2,1)S(1)}) custom-call(s32[1]{0:T(128)} %bitcast.4.z_ref, s32[1]{0:T(128)} %bitcast.5.core_ref, bf16[384,896]{1,0:T(8,128)(2,1)S(1)} %bitcast.18, bf16[1,896]{1,0:T(2,128)(2,1)S(1)} %broadcast_in_dim.15.gain_ref, ...), custom_call_target="tpu_custom_call" | custom-call | flops 10000000000 | bytes 10000000 | tf_op jit(solution)/shard_map/up_part/pallas_call | solution.py:374
  71.3 1.4 %collective-permute-start.4 = (bf16[880,128]{1,0:T(8,128)(2,1)S(1)}, bf16[880,128]{1,0:T(8,128)(2,1)S(1)}, u32[]{:S(2)}, u32[]{:S(2)}) collective-permute-start(bf16[880,128]{1,0:T(8,128)(2,1)S(1)} %add.8), channel_id=1, source_target_pairs={{0,64},{64,0},{128,192},{192,128},{1,65},{65,1},{129,193},{193,129... | collective-permute-start | bytes 675848 | tf_op jit(solution)/shard_map/ppermute | solution.py:504
  72.8 1.7 %collective-permute-done.5.refs_1_ = bf16[880,128]{1,0:T(8,128)(2,1)S(1)} collective-permute-done((bf16[880,128]{1,0:T(8,128)(2,1)S(1)}, bf16[880,128]{1,0:T(8,128)(2,1)S(1)}, u32[]{:S(2)}, u32[]{:S(2)}) %collective-permute-start.5) | collective-permute-done | bytes 225312 | tf_op jit(solution)/shard_map/ppermute | solution.py:508
  74.5 4.6 %collective-permute-done.6.refs_2_ = bf16[880,128]{1,0:T(8,128)(2,1)S(1)} collective-permute-done((bf16[880,128]{1,0:T(8,128)(2,1)S(1)}, bf16[880,128]{1,0:T(8,128)(2,1)S(1)}, u32[]{:S(2)}, u32[]{:S(2)}) %collective-permute-start.6) | collective-permute-done | bytes 225312 | tf_op jit(solution)/shard_map/ppermute | solution.py:504
  79.2 1.1 collective-permute-start.7
  80.3 2.8 %fetch.1 = (bf16[1152,896]{1,0:T(8,128)(2,1)S(1)}, bf16[1152,896]{1,0:T(8,128)(2,1)S(1)}) custom-call(bf16[1152,896]{1,0:T(8,128)(2,1)S(1)} %copy-done.4, bf16[1152,896]{1,0:T(8,128)(2,1)S(1)} %collective-permute-done.8.refs_1_), custom_call_target="tpu_custom_call" | custom-call | flops 10000000000 | bytes 10000000 | tf_op jit(solution)/shard_map/fetch/pallas_call | solution.py:274
  83.2 7.9 %collective-permute-done.7.refs_3_ = bf16[880,128]{1,0:T(8,128)(2,1)S(1)} collective-permute-done((bf16[880,128]{1,0:T(8,128)(2,1)S(1)}, bf16[880,128]{1,0:T(8,128)(2,1)S(1)}, u32[]{:S(2)}, u32[]{:S(2)}) %collective-permute-start.7) | collective-permute-done | bytes 225312 | tf_op jit(solution)/shard_map/ppermute | solution.py:504
  91.4 2.3 %collective-permute-start.9 = (bf16[48,1152]{1,0:T(8,128)(2,1)S(1)}, bf16[48,1152]{1,0:T(8,128)(2,1)S(1)}, u32[]{:S(2)}, u32[]{:S(2)}) collective-permute-start(bf16[48,1152]{1,0:T(8,128)(2,1)S(1)} %activate.1.refs_0_), channel_id=1, source_target_pairs={{0,64},{64,0},{128,192},{192,128},{1,65},{65,1},{129,193},{193,129... | collective-permute-start | bytes 331784 | tf_op jit(solution)/shard_map/ppermute | solution.py:504
  93.7 1.2 collective-permute-done.11.received_ref
  94.9 2.7 %collective-permute-done.10.refs_2_ = bf16[48,1152]{1,0:T(8,128)(2,1)S(1)} collective-permute-done((bf16[48,1152]{1,0:T(8,128)(2,1)S(1)}, bf16[48,1152]{1,0:T(8,128)(2,1)S(1)}, u32[]{:S(2)}, u32[]{:S(2)}) %collective-permute-start.10) | collective-permute-done | bytes 110624 | tf_op jit(solution)/shard_map/ppermute | solution.py:504
  97.7 0.9 down_most.1
  98.6 3.8 %collective-permute-done.12.rows_ref = bf16[48,1152]{1,0:T(8,128)(2,1)S(1)} collective-permute-done((bf16[48,1152]{1,0:T(8,128)(2,1)S(1)}, bf16[48,1152]{1,0:T(8,128)(2,1)S(1)}, u32[]{:S(2)}, u32[]{:S(2)}) %collective-permute-start.12) | collective-permute-done | bytes 110624 | tf_op jit(solution)/shard_map/ppermute | solution.py:504
  102.4 1.3 %down.1 = bf16[384,896]{1,0:T(8,128)(2,1)S(1)} custom-call(s32[1]{0:T(128)} %bitcast.4.z_ref, bf16[144,896]{1,0:T(8,128)(2,1)S(1)} %get-tuple-element.81.own_most_ref, bf16[144,896]{1,0:T(8,128)(2,1)S(1)} %get-tuple-element.82.other_most_ref, bf16[48,1152]{1,0:T(8,128)(2,1)S(1)} %collective-permute-done.12.rows_ref, ...), custom_call_target="tpu_custom_call" | custom-call | tf_op jit(solution)/shard_map/down/pallas_call | solution.py:247
  103.7 14.2 %all_to_all.23.parts_ref = bf16[16,24,896]{2,1,0:T(8,128)(2,1)S(1)} all-to-all(bf16[16,24,896]{2,1,0:T(8,128)(2,1)S(1)} %bitcast.13), channel_id=1, replica_groups=mesh['z'=4,'core'=2,'x'=4,'y'=4,'rep'=2] {'x','y'}, dimensions={0} | all-to-all | bytes 1376256 | tf_op jit(solution)/shard_map/all_to_all | solution.py:584
  118.4 2.1 %collective-permute-start.14 = (bf16[8,896]{1,0:T(8,128)(2,1)S(1)}, bf16[8,896]{1,0:T(8,128)(2,1)S(1)}, u32[]{:S(2)}, u32[]{:S(2)}) collective-permute-start(bf16[8,896]{1,0:T(8,128)(2,1)S(1)} %get-tuple-element.87), channel_id=1, source_target_pairs={{0,128},{64,192},{128,0},{192,64},{1,129},{65,193},{129,1},{193,65... | collective-permute-start | bytes 43016 | tf_op jit(solution)/shard_map/ppermute | solution.py:504
  120.5 2.3 %collective-permute-start.15 = (bf16[8,896]{1,0:T(8,128)(2,1)S(1)}, bf16[8,896]{1,0:T(8,128)(2,1)S(1)}, u32[]{:S(2)}, u32[]{:S(2)}) collective-permute-start(bf16[8,896]{1,0:T(8,128)(2,1)S(1)} %get-tuple-element.88), channel_id=1, source_target_pairs={{0,192},{64,128},{128,64},{192,0},{1,193},{65,129},{129,65},{193,1... | collective-permute-start | bytes 43016 | tf_op jit(solution)/shard_map/ppermute | solution.py:504
  123.1 2.9 %collective-permute-done.15.refs_3_ = bf16[8,896]{1,0:T(8,128)(2,1)S(1)} collective-permute-done((bf16[8,896]{1,0:T(8,128)(2,1)S(1)}, bf16[8,896]{1,0:T(8,128)(2,1)S(1)}, u32[]{:S(2)}, u32[]{:S(2)}) %collective-permute-start.15) | collective-permute-done | bytes 14368 | tf_op jit(solution)/shard_map/ppermute | solution.py:504
  (41 shorter events, 5.0 us)
Async XLA Ops:
  0.0 30.6 %copy-start = (bf16[1024,896]{1,0:T(8,128)(2,1)S(1)}, bf16[1024,896]{1,0:T(8,128)(2,1)}, u32[]{:S(2)}) copy-start(bf16[1024,896]{1,0:T(8,128)(2,1)} %weight_ref.3) | copy-start | bytes 5505028
  30.5 0.7 copy-start.5
  30.5 1.8 %collective-permute-start = (bf16[192,1024]{1,0:T(8,128)(2,1)S(1)}, bf16[192,1024]{1,0:T(8,128)(2,1)S(1)}, u32[]{:S(2)}, u32[]{:S(2)}) collective-permute-start(bf16[192,1024]{1,0:T(8,128)(2,1)S(1)} %to_rows.1.rows_ref), channel_id=1, source_target_pairs={{0,32},{32,0},{1,33},{33,1},{2,34},{34,2},{3,35},{35,3},{4,36},{36... | collective-permute-start | bytes 1179656 | tf_op jit(solution)/shard_map/ppermute | solution.py:508
  31.3 19.0 %copy-start.1 = (bf16[3,128,896]{2,1,0:T(8,128)(2,1)S(1)}, bf16[3,128,896]{2,1,0:T(8,128)(2,1)}, u32[]{:S(2)}) copy-start(bf16[3,128,896]{2,1,0:T(8,128)(2,1)} %param.11) | copy-start | bytes 2064388
  33.5 32.8 %copy-start.2 = (bf16[896,1152]{1,0:T(8,128)(2,1)S(1)}, bf16[896,1152]{1,0:T(8,128)(2,1)}, u32[]{:S(2)}) copy-start(bf16[896,1152]{1,0:T(8,128)(2,1)} %gate_ref.3) | copy-start | bytes 6193156
  33.5 32.8 %copy-start.3 = (bf16[896,1152]{1,0:T(8,128)(2,1)S(1)}, bf16[896,1152]{1,0:T(8,128)(2,1)}, u32[]{:S(2)}) copy-start(bf16[896,1152]{1,0:T(8,128)(2,1)} %up_ref.3) | copy-start | bytes 6193156
  67.8 2.1 %collective-permute-start.1 = (bf16[880,128]{1,0:T(8,128)(2,1)S(1)}, bf16[880,128]{1,0:T(8,128)(2,1)S(1)}, u32[]{:S(2)}, u32[]{:S(2)}) collective-permute-start(bf16[880,128]{1,0:T(8,128)(2,1)S(1)} %get-tuple-element.57), channel_id=1, source_target_pairs={{0,32},{32,0},{1,33},{33,1},{2,34},{34,2},{3,35},{35,3},{4,36},{36... | collective-permute-start | bytes 675848 | tf_op jit(solution)/shard_map/ppermute | solution.py:508
  67.9 2.1 %copy-start.4 = (bf16[1152,896]{1,0:T(8,128)(2,1)S(1)}, bf16[1152,896]{1,0:T(8,128)(2,1)}, u32[]{:S(2)}) copy-start(bf16[1152,896]{1,0:T(8,128)(2,1)} %refs_0_) | copy-start | bytes 6193156
  67.9 2.0 %collective-permute-start.2 = (bf16[880,128]{1,0:T(8,128)(2,1)S(1)}, bf16[880,128]{1,0:T(8,128)(2,1)S(1)}, u32[]{:S(2)}, u32[]{:S(2)}) collective-permute-start(bf16[880,128]{1,0:T(8,128)(2,1)S(1)} %get-tuple-element.58), channel_id=1, source_target_pairs={{0,32},{32,0},{1,33},{33,1},{2,34},{34,2},{3,35},{35,3},{4,36},{36... | collective-permute-start | bytes 675848 | tf_op jit(solution)/shard_map/ppermute | solution.py:508
  70.0 10.3 %collective-permute-start.8 = (bf16[1152,896]{1,0:T(8,128)(2,1)S(1)}, bf16[1152,896]{1,0:T(8,128)(2,1)S(1)}, u32[]{:S(2)}, u32[]{:S(2)}) collective-permute-start(bf16[1152,896]{1,0:T(8,128)(2,1)S(1)} %copy-done.4), channel_id=1, source_target_pairs={{0,32},{32,0},{1,33},{33,1},{2,34},{34,2},{3,35},{35,3},{4,36},{36... | collective-permute-start | bytes 6193160 | tf_op jit(solution)/shard_map/ppermute | solution.py:508
  70.2 4.3 %collective-permute-start.5 = (bf16[880,128]{1,0:T(8,128)(2,1)S(1)}, bf16[880,128]{1,0:T(8,128)(2,1)S(1)}, u32[]{:S(2)}, u32[]{:S(2)}) collective-permute-start(bf16[880,128]{1,0:T(8,128)(2,1)S(1)} %get-tuple-element.69), channel_id=1, source_target_pairs={{0,32},{32,0},{1,33},{33,1},{2,34},{34,2},{3,35},{35,3},{4,36},{36... | collective-permute-start | bytes 675848 | tf_op jit(solution)/shard_map/ppermute | solution.py:508
  70.7 8.4 %collective-permute-start.6 = (bf16[880,128]{1,0:T(8,128)(2,1)S(1)}, bf16[880,128]{1,0:T(8,128)(2,1)S(1)}, u32[]{:S(2)}, u32[]{:S(2)}) collective-permute-start(bf16[880,128]{1,0:T(8,128)(2,1)S(1)} %add.7), channel_id=1, source_target_pairs={{0,64},{64,0},{128,192},{192,128},{1,65},{65,1},{129,193},{193,129... | collective-permute-start | bytes 675848 | tf_op jit(solution)/shard_map/ppermute | solution.py:504
  71.3 19.8 %collective-permute-start.4 = (bf16[880,128]{1,0:T(8,128)(2,1)S(1)}, bf16[880,128]{1,0:T(8,128)(2,1)S(1)}, u32[]{:S(2)}, u32[]{:S(2)}) collective-permute-start(bf16[880,128]{1,0:T(8,128)(2,1)S(1)} %add.8), channel_id=1, source_target_pairs={{0,64},{64,0},{128,192},{192,128},{1,65},{65,1},{129,193},{193,129... | collective-permute-start | bytes 675848 | tf_op jit(solution)/shard_map/ppermute | solution.py:504
  72.8 18.3 %collective-permute-start.3 = (bf16[880,128]{1,0:T(8,128)(2,1)S(1)}, bf16[880,128]{1,0:T(8,128)(2,1)S(1)}, u32[]{:S(2)}, u32[]{:S(2)}) collective-permute-start(bf16[880,128]{1,0:T(8,128)(2,1)S(1)} %get-tuple-element.65), channel_id=1, source_target_pairs={{0,32},{32,0},{1,33},{33,1},{2,34},{34,2},{3,35},{35,3},{4,36},{36... | collective-permute-start | bytes 675848 | tf_op jit(solution)/shard_map/ppermute | solution.py:508
  79.2 11.9 %collective-permute-start.7 = (bf16[880,128]{1,0:T(8,128)(2,1)S(1)}, bf16[880,128]{1,0:T(8,128)(2,1)S(1)}, u32[]{:S(2)}, u32[]{:S(2)}) collective-permute-start(bf16[880,128]{1,0:T(8,128)(2,1)S(1)} %add.9), channel_id=1, source_target_pairs={{0,128},{64,192},{128,0},{192,64},{1,129},{65,193},{129,1},{193,65... | collective-permute-start | bytes 675848 | tf_op jit(solution)/shard_map/ppermute | solution.py:504
  91.3 6.3 %collective-permute-start.10 = (bf16[48,1152]{1,0:T(8,128)(2,1)S(1)}, bf16[48,1152]{1,0:T(8,128)(2,1)S(1)}, u32[]{:S(2)}, u32[]{:S(2)}) collective-permute-start(bf16[48,1152]{1,0:T(8,128)(2,1)S(1)} %activate.1.refs_0_), channel_id=1, source_target_pairs={{0,128},{64,192},{128,0},{192,64},{1,129},{65,193},{129,1},{193,65... | collective-permute-start | bytes 331784 | tf_op jit(solution)/shard_map/ppermute | solution.py:504
  91.4 6.3 %collective-permute-start.9 = (bf16[48,1152]{1,0:T(8,128)(2,1)S(1)}, bf16[48,1152]{1,0:T(8,128)(2,1)S(1)}, u32[]{:S(2)}, u32[]{:S(2)}) collective-permute-start(bf16[48,1152]{1,0:T(8,128)(2,1)S(1)} %activate.1.refs_0_), channel_id=1, source_target_pairs={{0,64},{64,0},{128,192},{192,128},{1,65},{65,1},{129,193},{193,129... | collective-permute-start | bytes 331784 | tf_op jit(solution)/shard_map/ppermute | solution.py:504
  93.7 1.2 collective-permute-start.11
  97.7 4.7 %collective-permute-start.12 = (bf16[48,1152]{1,0:T(8,128)(2,1)S(1)}, bf16[48,1152]{1,0:T(8,128)(2,1)S(1)}, u32[]{:S(2)}, u32[]{:S(2)}) collective-permute-start(bf16[48,1152]{1,0:T(8,128)(2,1)S(1)} %collective-permute-done.10.refs_2_), channel_id=1, source_target_pairs={{0,64},{64,0},{128,192},{192,128},{1,65},{65,1},{129,193},{193,129... | collective-permute-start | bytes 331784 | tf_op jit(solution)/shard_map/ppermute | solution.py:504
  118.3 4.5 %collective-permute-start.13 = (bf16[8,896]{1,0:T(8,128)(2,1)S(1)}, bf16[8,896]{1,0:T(8,128)(2,1)S(1)}, u32[]{:S(2)}, u32[]{:S(2)}) collective-permute-start(bf16[8,896]{1,0:T(8,128)(2,1)S(1)} %get-tuple-element.86), channel_id=1, source_target_pairs={{0,64},{64,0},{128,192},{192,128},{1,65},{65,1},{129,193},{193,129... | collective-permute-start | bytes 43016 | tf_op jit(solution)/shard_map/ppermute | solution.py:504
  118.4 4.7 %collective-permute-start.14 = (bf16[8,896]{1,0:T(8,128)(2,1)S(1)}, bf16[8,896]{1,0:T(8,128)(2,1)S(1)}, u32[]{:S(2)}, u32[]{:S(2)}) collective-permute-start(bf16[8,896]{1,0:T(8,128)(2,1)S(1)} %get-tuple-element.87), channel_id=1, source_target_pairs={{0,128},{64,192},{128,0},{192,64},{1,129},{65,193},{129,1},{193,65... | collective-permute-start | bytes 43016 | tf_op jit(solution)/shard_map/ppermute | solution.py:504
  120.5 5.5 %collective-permute-start.15 = (bf16[8,896]{1,0:T(8,128)(2,1)S(1)}, bf16[8,896]{1,0:T(8,128)(2,1)S(1)}, u32[]{:S(2)}, u32[]{:S(2)}) collective-permute-start(bf16[8,896]{1,0:T(8,128)(2,1)S(1)} %get-tuple-element.88), channel_id=1, source_target_pairs={{0,192},{64,128},{128,64},{192,0},{1,193},{65,129},{129,65},{193,1... | collective-permute-start | bytes 43016 | tf_op jit(solution)/shard_map/ppermute | solution.py:504

commit v2 on v1

--- a/solution.py
+++ b/solution.py
@@ -80,29 +80,34 @@
     pieces = head_dim // LANES
     group = heads // blocks
     positions = lax.broadcasted_iota(jnp.int32, (heads, pos), 1)
+    requests = []
+    scores = []
+    for s in range(slot_count):
+        request = micro - 1
+        for m in range(micro - 1):
+            request = jnp.where(slots[0, m] == s, m, request)
+        requests.append(request)
+        query = wide[request].astype(BF16)
+        key_copies[s].wait()
+        scores.append(lax.dot_general(query, keys[s], (((1,), (1,)), ((), ())), preferred_element_type=F32))
     softened = []
     totals = []
-    for copy in key_copies:
-        copy.wait()
-    for m in range(micro):
-        scores = lax.dot_general(
-            wide[m].astype(BF16), keys[slots[0, m]], (((1,), (1,)), ((), ())), preferred_element_type=F32
-        ) * head_dim ** (-0.5)
-        in_cache = positions < lengths[0, m]
-        scores = jnp.where(in_cache, scores, MASKED)
-        highest = jnp.max(scores, axis=1, keepdims=True)
-        weights = jnp.where(in_cache, jnp.exp(scores - highest), 0.0)
+    for s in range(slot_count):
+        in_cache = positions < lengths[0, requests[s]]
+        masked = jnp.where(in_cache, scores[s] * head_dim ** (-0.5), MASKED)
+        highest = jnp.max(masked, axis=1, keepdims=True)
+        weights = jnp.where(in_cache, jnp.exp(masked - highest), 0.0)
         totals.append(jnp.sum(weights, axis=1, keepdims=True))
         softened.append(weights.astype(BF16))
     for copy in value_copies:
         copy.wait()
-    for m in range(micro):
-        weighted = jnp.dot(softened[m], values[slots[0, m]], preferred_element_type=F32)
-        attended = weighted / totals[m]
+    for s in range(slot_count):
+        weighted = jnp.dot(softened[s], values[s], preferred_element_type=F32)
+        attended = weighted / totals[s]
         for piece in range(pieces):
             part = attended[:, piece * LANES : (piece + 1) * LANES].reshape(blocks, group, LANES).astype(BF16)
             for copy in range(copies):
-                out_ref[copy, :, m, piece * group : (piece + 1) * group, :] = part
+                out_ref[copy, :, requests[s], piece * group : (piece + 1) * group, :] = part
 
 
 def attend(queries, key_cache, value_cache, slots, lengths, z_count, ffn_count):
@@ -167,44 +172,46 @@
     )(tiles)
 
 
-def product_kernel(rows_ref, weight_ref, out_ref):
-    out_ref[...] = jnp.dot(rows_ref[...], weight_ref[...], preferred_element_type=F32).astype(BF16)
-
-
-def product_of(rows, weight):
-    return pl.pallas_call(
-        product_kernel,
-        out_shape=jax.ShapeDtypeStruct((rows.shape[0], weight.shape[1]), BF16),
-        in_specs=[whole(), whole()],
-        out_specs=whole(),
-        compiler_params=params(12),
-        cost_estimate=HEAVY,
-        name="product",
-    )(rows, weight)
-
-
-def mix_kernel(order, core_ref, own_ref, rows_ref, weight_ref, out_ref):
+def mixed_rows(order, core, rows_ref, weight_ref):
     z_count, core_count, ffn_count, micro = order
-    total = 2 * rows_ref.shape[0]
     product = jnp.dot(rows_ref[...], weight_ref[...], preferred_element_type=F32).astype(BF16)
-    core = core_ref[0]
 
     def source(r):
         m = r % micro
         c = (r // micro) % core_count
         z = (r // (micro * core_count)) % z_count
         f = r // (micro * core_count * z_count)
-        return (((c ^ core) * z_count + z) * ffn_count + f) * micro + m
-
-    spread = one_hot((total, total), source).astype(BF16)
-    both = jnp.concatenate([own_ref[...], product], axis=0)
-    out_ref[...] = jnp.dot(spread, both, preferred_element_type=F32).astype(BF16)
+        return jnp.where(c == core, (z * ffn_count + f) * micro + m, -1)
+
+    spread = one_hot((core_count * product.shape[0], product.shape[0]), source).astype(BF16)
+    return jnp.dot(spread, product, preferred_element_type=F32)
+
+
+def product_kernel(order, core_ref, rows_ref, weight_ref, out_ref):
+    out_ref[...] = mixed_rows(order, core_ref[0], rows_ref, weight_ref).astype(BF16)
+
+
+def product_of(core, rows, weight, order):
+    return pl.pallas_call(
+        functools.partial(product_kernel, order),
+        out_shape=jax.ShapeDtypeStruct((2 * rows.shape[0], weight.shape[1]), BF16),
+        in_specs=[scalars(), whole(), whole()],
+        out_specs=whole(),
+        compiler_params=params(12),
+        cost_estimate=HEAVY,
+        name="product",
+    )(core, rows, weight)
+
+
+def mix_kernel(order, core_ref, own_ref, rows_ref, weight_ref, out_ref):
+    other = mixed_rows(order, 1 - core_ref[0], rows_ref, weight_ref)
+    out_ref[...] = (own_ref[...].astype(F32) + other).astype(BF16)
 
 
 def mix(core, own, rows, weight, order):
     return pl.pallas_call(
         functools.partial(mix_kernel, order),
-        out_shape=jax.ShapeDtypeStruct((2 * rows.shape[0], weight.shape[1]), BF16),
+        out_shape=jax.ShapeDtypeStruct(own.shape, BF16),
         in_specs=[scalars(), whole(), whole(), whole()],
         out_specs=whole(),
         compiler_params=params(12),
@@ -548,7 +555,7 @@
     own_rows, ffn_gain = lax.optimization_barrier((own_rows, ffn_gain))
     other_rows = swap_cores(own_rows)
     gain = ffn_gain[None, :]
-    own_mixed = product_of(own_rows, out_weight)
+    own_mixed = product_of(core_index, own_rows, out_weight, order)
     own_mixed, other_rows, gain = lax.optimization_barrier((own_mixed, other_rows, gain))
     mixed = mix(core_index, own_mixed, other_rows, out_weight, order)
 

time: 127 us -> 126 us (level)
  no operation moved by 1% of the time
where the time goes in v2:
time: 126 us
  blocking collectives  72.9 us (58%)
  waiting for transfers between devices  26 us (21%)
  Pallas kernels  15.6 us (12%)
  starting transfers between devices  11.2 us (9%)
    all_to_all x1, blocking collectives, per_device(): lax.all_to_all(payload, (Z,) + FFN, split_axis=0, concat_axis=0, tiled=True)  26.3 us
    ppermute x9, waiting for transfers between devices, along_z(): lax.ppermute(array, Z, [(i, i ^ hop) for i in range(lax.axis_size(Z))])  22.3 us
    all_to_all x1, blocking collectives, per_device(): lax.all_to_all(mixed.reshape(ffn_count, rows_chunk, col_share), FFN, spli...  16.8 us
    all_to_all x1, blocking collectives, per_device(): lax.all_to_all(copies, FFN, split_axis=0, concat_axis=0, tiled=True)  15.6 us
    all_to_all x1, blocking collectives, per_device(): lax.all_to_all(lowered.reshape(ffn_count, rows_chunk, col_share), FFN, sp...  14.2 us
    ppermute x9, starting transfers between devices, along_z(): lax.ppermute(array, Z, [(i, i ^ hop) for i in range(lax.axis_size(Z))])  9.83 us
    pallas_call x1, Pallas kernels, attend(): pl.pallas_call(attention_kernel, in_specs=[in_hbm()] * 5, out_specs=whole...  3.66 us
    ppermute x7, waiting for transfers between devices, swap_cores(): return lax.ppermute(array, CORE, [(0, 1), (1, 0)])  3.64 us
  transfers between devices with their start and end apart: 16, of which 9 were waited for; matrix products, arithmetic and copies ran while one was open for 0% of the time, Pallas kernels for 5%

profile of v2, /device:TPU:8, one launch (start us, length us, event | category | flops | bytes accessed | tf_op | source)
XLA Modules:
  0.0 126.0 jit_solution(15832499919255356408)
XLA Ops:
  0.0 3.7 %attention.1 = bf16[4,16,3,8,128]{4,3,2,1,0:T(8,128)(2,1)} custom-call(s32[1,3]{1,0:T(1,128)} %bitcast.21, s32[1,3]{1,0:T(1,128)} %bitcast.22, bf16[3,16384]{1,0:T(4,128)(2,1)} %bitcast.20, bf16[3,1024,256]{2,1,0:T(8,128)(2,1)} %key_hbm.1, bf16[3,1024,256]{2,1,0:T(8,128)(2,1)} %value_hbm.1), custom_call_target="tpu_custom_call" | custom-call | tf_op jit(solution)/shard_map/attention/pallas_call | solution.py:117
  3.7 26.3 %all_to_all.20 = bf16[64,24,128]{2,1,0:T(8,128)(2,1)S(1)} all-to-all(bf16[64,24,128]{2,1,0:T(8,128)(2,1)} %bitcast.19), channel_id=1, replica_groups=mesh['z'=4,'core'=2,'x'=4,'y'=4,'rep'=2] {'z','x','y'}, dimensions={0} | all-to-all | bytes 786432 | tf_op jit(solution)/shard_map/all_to_all | solution.py:553
  30.3 1.0 product.1.own_ref
  32.0 1.0 mix.1
  33.0 16.8 %all_to_all.21.parts_ref = bf16[16,24,896]{2,1,0:T(8,128)(2,1)S(1)} all-to-all(bf16[16,24,896]{2,1,0:T(8,128)(2,1)S(1)} %bitcast.14), channel_id=1, replica_groups=mesh['z'=4,'core'=2,'x'=4,'y'=4,'rep'=2] {'x','y'}, dimensions={0} | all-to-all | bytes 1376256 | tf_op jit(solution)/shard_map/all_to_all | solution.py:562
  50.2 15.6 %all_to_all.22 = bf16[16,24,896]{2,1,0:T(8,128)(2,1)S(1)} all-to-all(bf16[16,24,896]{2,1,0:T(8,128)(2,1)S(1)} %get-tuple-element.55), channel_id=1, replica_groups=mesh['z'=4,'core'=2,'x'=4,'y'=4,'rep'=2] {'x','y'}, dimensions={0} | all-to-all | bytes 1376256 | tf_op jit(solution)/shard_map/all_to_all | solution.py:566
  65.8 1.5 %up_part.2 = (bf16[880,128]{1,0:T(8,128)(2,1)S(1)}, bf16[880,128]{1,0:T(8,128)(2,1)S(1)}, bf16[880,128]{1,0:T(8,128)(2,1)S(1)}, bf16[880,128]{1,0:T(8,128)(2,1)S(1)}) custom-call(s32[1]{0:T(128)} %bitcast.4.z_ref, s32[1]{0:T(128)} %bitcast.5.core_ref, bf16[384,896]{1,0:T(8,128)(2,1)S(1)} %bitcast.17, bf16[1,896]{1,0:T(2,128)(2,1)S(1)} %broadcast_in_dim.15.gain_ref, ...), custom_call_target="tpu_custom_call" | custom-call | flops 10000000000 | bytes 10000000 | tf_op jit(solution)/shard_map/up_part/pallas_call | solution.py:381
  67.9 1.5 %up_part.3 = (bf16[880,128]{1,0:T(8,128)(2,1)S(1)}, bf16[880,128]{1,0:T(8,128)(2,1)S(1)}, bf16[880,128]{1,0:T(8,128)(2,1)S(1)}, bf16[880,128]{1,0:T(8,128)(2,1)S(1)}) custom-call(s32[1]{0:T(128)} %bitcast.4.z_ref, s32[1]{0:T(128)} %bitcast.5.core_ref, bf16[384,896]{1,0:T(8,128)(2,1)S(1)} %bitcast.18, bf16[1,896]{1,0:T(2,128)(2,1)S(1)} %broadcast_in_dim.15.gain_ref, ...), custom_call_target="tpu_custom_call" | custom-call | flops 10000000000 | bytes 10000000 | tf_op jit(solution)/shard_map/up_part/pallas_call | solution.py:381
  70.8 1.4 %collective-permute-start.4 = (bf16[880,128]{1,0:T(8,128)(2,1)S(1)}, bf16[880,128]{1,0:T(8,128)(2,1)S(1)}, u32[]{:S(2)}, u32[]{:S(2)}) collective-permute-start(bf16[880,128]{1,0:T(8,128)(2,1)S(1)} %add.8), channel_id=1, source_target_pairs={{0,64},{64,0},{128,192},{192,128},{1,65},{65,1},{129,193},{193,129... | collective-permute-start | bytes 675848 | tf_op jit(solution)/shard_map/ppermute | solution.py:511
  72.3 1.7 %collective-permute-done.5.refs_1_ = bf16[880,128]{1,0:T(8,128)(2,1)S(1)} collective-permute-done((bf16[880,128]{1,0:T(8,128)(2,1)S(1)}, bf16[880,128]{1,0:T(8,128)(2,1)S(1)}, u32[]{:S(2)}, u32[]{:S(2)}) %collective-permute-start.5) | collective-permute-done | bytes 225312 | tf_op jit(solution)/shard_map/ppermute | solution.py:515
  74.0 4.6 %collective-permute-done.6.refs_2_ = bf16[880,128]{1,0:T(8,128)(2,1)S(1)} collective-permute-done((bf16[880,128]{1,0:T(8,128)(2,1)S(1)}, bf16[880,128]{1,0:T(8,128)(2,1)S(1)}, u32[]{:S(2)}, u32[]{:S(2)}) %collective-permute-start.6) | collective-permute-done | bytes 225312 | tf_op jit(solution)/shard_map/ppermute | solution.py:511
  78.7 1.0 collective-permute-start.7
  79.7 2.8 %fetch.1 = (bf16[1152,896]{1,0:T(8,128)(2,1)S(1)}, bf16[1152,896]{1,0:T(8,128)(2,1)S(1)}) custom-call(bf16[1152,896]{1,0:T(8,128)(2,1)S(1)} %copy-done.4, bf16[1152,896]{1,0:T(8,128)(2,1)S(1)} %collective-permute-done.8.refs_1_), custom_call_target="tpu_custom_call" | custom-call | flops 10000000000 | bytes 10000000 | tf_op jit(solution)/shard_map/fetch/pallas_call | solution.py:281
  82.5 7.9 %collective-permute-done.7.refs_3_ = bf16[880,128]{1,0:T(8,128)(2,1)S(1)} collective-permute-done((bf16[880,128]{1,0:T(8,128)(2,1)S(1)}, bf16[880,128]{1,0:T(8,128)(2,1)S(1)}, u32[]{:S(2)}, u32[]{:S(2)}) %collective-permute-start.7) | collective-permute-done | bytes 225312 | tf_op jit(solution)/shard_map/ppermute | solution.py:511
  90.7 2.2 %collective-permute-start.9 = (bf16[48,1152]{1,0:T(8,128)(2,1)S(1)}, bf16[48,1152]{1,0:T(8,128)(2,1)S(1)}, u32[]{:S(2)}, u32[]{:S(2)}) collective-permute-start(bf16[48,1152]{1,0:T(8,128)(2,1)S(1)} %activate.1.refs_0_), channel_id=1, source_target_pairs={{0,64},{64,0},{128,192},{192,128},{1,65},{65,1},{129,193},{193,129... | collective-permute-start | bytes 331784 | tf_op jit(solution)/shard_map/ppermute | solution.py:511
  93.0 1.2 collective-permute-done.11.received_ref
  94.2 2.7 %collective-permute-done.10.refs_2_ = bf16[48,1152]{1,0:T(8,128)(2,1)S(1)} collective-permute-done((bf16[48,1152]{1,0:T(8,128)(2,1)S(1)}, bf16[48,1152]{1,0:T(8,128)(2,1)S(1)}, u32[]{:S(2)}, u32[]{:S(2)}) %collective-permute-start.10) | collective-permute-done | bytes 110624 | tf_op jit(solution)/shard_map/ppermute | solution.py:511
  96.9 1.0 down_most.1
  97.9 3.8 %collective-permute-done.12.rows_ref = bf16[48,1152]{1,0:T(8,128)(2,1)S(1)} collective-permute-done((bf16[48,1152]{1,0:T(8,128)(2,1)S(1)}, bf16[48,1152]{1,0:T(8,128)(2,1)S(1)}, u32[]{:S(2)}, u32[]{:S(2)}) %collective-permute-start.12) | collective-permute-done | bytes 110624 | tf_op jit(solution)/shard_map/ppermute | solution.py:511
  101.6 1.3 %down.1 = bf16[384,896]{1,0:T(8,128)(2,1)S(1)} custom-call(s32[1]{0:T(128)} %bitcast.4.z_ref, bf16[144,896]{1,0:T(8,128)(2,1)S(1)} %get-tuple-element.81.own_most_ref, bf16[144,896]{1,0:T(8,128)(2,1)S(1)} %get-tuple-element.82.other_most_ref, bf16[48,1152]{1,0:T(8,128)(2,1)S(1)} %collective-permute-done.12.rows_ref, ...), custom_call_target="tpu_custom_call" | custom-call | tf_op jit(solution)/shard_map/down/pallas_call | solution.py:254
  103.0 14.2 %all_to_all.23.parts_ref = bf16[16,24,896]{2,1,0:T(8,128)(2,1)S(1)} all-to-all(bf16[16,24,896]{2,1,0:T(8,128)(2,1)S(1)} %bitcast.13), channel_id=1, replica_groups=mesh['z'=4,'core'=2,'x'=4,'y'=4,'rep'=2] {'x','y'}, dimensions={0} | all-to-all | bytes 1376256 | tf_op jit(solution)/shard_map/all_to_all | solution.py:591
  117.6 2.2 %collective-permute-start.14 = (bf16[8,896]{1,0:T(8,128)(2,1)S(1)}, bf16[8,896]{1,0:T(8,128)(2,1)S(1)}, u32[]{:S(2)}, u32[]{:S(2)}) collective-permute-start(bf16[8,896]{1,0:T(8,128)(2,1)S(1)} %get-tuple-element.87), channel_id=1, source_target_pairs={{0,128},{64,192},{128,0},{192,64},{1,129},{65,193},{129,1},{193,65... | collective-permute-start | bytes 43016 | tf_op jit(solution)/shard_map/ppermute | solution.py:511
  119.8 2.2 %collective-permute-start.15 = (bf16[8,896]{1,0:T(8,128)(2,1)S(1)}, bf16[8,896]{1,0:T(8,128)(2,1)S(1)}, u32[]{:S(2)}, u32[]{:S(2)}) collective-permute-start(bf16[8,896]{1,0:T(8,128)(2,1)S(1)} %get-tuple-element.88), channel_id=1, source_target_pairs={{0,192},{64,128},{128,64},{192,0},{1,193},{65,129},{129,65},{193,1... | collective-permute-start | bytes 43016 | tf_op jit(solution)/shard_map/ppermute | solution.py:511
  122.3 3.0 %collective-permute-done.15.refs_3_ = bf16[8,896]{1,0:T(8,128)(2,1)S(1)} collective-permute-done((bf16[8,896]{1,0:T(8,128)(2,1)S(1)}, bf16[8,896]{1,0:T(8,128)(2,1)S(1)}, u32[]{:S(2)}, u32[]{:S(2)}) %collective-permute-start.15) | collective-permute-done | bytes 14368 | tf_op jit(solution)/shard_map/ppermute | solution.py:511
  (41 shorter events, 5.2 us)
Async XLA Ops:
  0.0 30.3 %copy-start = (bf16[1024,896]{1,0:T(8,128)(2,1)S(1)}, bf16[1024,896]{1,0:T(8,128)(2,1)}, u32[]{:S(2)}) copy-start(bf16[1024,896]{1,0:T(8,128)(2,1)} %weight_ref.3) | copy-start | bytes 5505028
  30.2 1.1 copy-start.5
  30.2 1.8 %collective-permute-start = (bf16[192,1024]{1,0:T(8,128)(2,1)S(1)}, bf16[192,1024]{1,0:T(8,128)(2,1)S(1)}, u32[]{:S(2)}, u32[]{:S(2)}) collective-permute-start(bf16[192,1024]{1,0:T(8,128)(2,1)S(1)} %to_rows.1.rows_ref), channel_id=1, source_target_pairs={{0,32},{32,0},{1,33},{33,1},{2,34},{34,2},{3,35},{35,3},{4,36},{36... | collective-permute-start | bytes 1179656 | tf_op jit(solution)/shard_map/ppermute | solution.py:515
  31.3 18.5 %copy-start.1 = (bf16[3,128,896]{2,1,0:T(8,128)(2,1)S(1)}, bf16[3,128,896]{2,1,0:T(8,128)(2,1)}, u32[]{:S(2)}) copy-start(bf16[3,128,896]{2,1,0:T(8,128)(2,1)} %param.11) | copy-start | bytes 2064388
  33.0 32.8 %copy-start.2 = (bf16[896,1152]{1,0:T(8,128)(2,1)S(1)}, bf16[896,1152]{1,0:T(8,128)(2,1)}, u32[]{:S(2)}) copy-start(bf16[896,1152]{1,0:T(8,128)(2,1)} %gate_ref.3) | copy-start | bytes 6193156
  33.0 32.8 %copy-start.3 = (bf16[896,1152]{1,0:T(8,128)(2,1)S(1)}, bf16[896,1152]{1,0:T(8,128)(2,1)}, u32[]{:S(2)}) copy-start(bf16[896,1152]{1,0:T(8,128)(2,1)} %up_ref.3) | copy-start | bytes 6193156
  67.3 2.1 %collective-permute-start.1 = (bf16[880,128]{1,0:T(8,128)(2,1)S(1)}, bf16[880,128]{1,0:T(8,128)(2,1)S(1)}, u32[]{:S(2)}, u32[]{:S(2)}) collective-permute-start(bf16[880,128]{1,0:T(8,128)(2,1)S(1)} %get-tuple-element.57), channel_id=1, source_target_pairs={{0,32},{32,0},{1,33},{33,1},{2,34},{34,2},{3,35},{35,3},{4,36},{36... | collective-permute-start | bytes 675848 | tf_op jit(solution)/shard_map/ppermute | solution.py:515
  67.4 2.1 %copy-start.4 = (bf16[1152,896]{1,0:T(8,128)(2,1)S(1)}, bf16[1152,896]{1,0:T(8,128)(2,1)}, u32[]{:S(2)}) copy-start(bf16[1152,896]{1,0:T(8,128)(2,1)} %refs_0_) | copy-start | bytes 6193156
  67.4 2.0 %collective-permute-start.2 = (bf16[880,128]{1,0:T(8,128)(2,1)S(1)}, bf16[880,128]{1,0:T(8,128)(2,1)S(1)}, u32[]{:S(2)}, u32[]{:S(2)}) collective-permute-start(bf16[880,128]{1,0:T(8,128)(2,1)S(1)} %get-tuple-element.58), channel_id=1, source_target_pairs={{0,32},{32,0},{1,33},{33,1},{2,34},{34,2},{3,35},{35,3},{4,36},{36... | collective-permute-start | bytes 675848 | tf_op jit(solution)/shard_map/ppermute | solution.py:515
  69.5 10.2 %collective-permute-start.8 = (bf16[1152,896]{1,0:T(8,128)(2,1)S(1)}, bf16[1152,896]{1,0:T(8,128)(2,1)S(1)}, u32[]{:S(2)}, u32[]{:S(2)}) collective-permute-start(bf16[1152,896]{1,0:T(8,128)(2,1)S(1)} %copy-done.4), channel_id=1, source_target_pairs={{0,32},{32,0},{1,33},{33,1},{2,34},{34,2},{3,35},{35,3},{4,36},{36... | collective-permute-start | bytes 6193160 | tf_op jit(solution)/shard_map/ppermute | solution.py:515
  69.7 4.3 %collective-permute-start.5 = (bf16[880,128]{1,0:T(8,128)(2,1)S(1)}, bf16[880,128]{1,0:T(8,128)(2,1)S(1)}, u32[]{:S(2)}, u32[]{:S(2)}) collective-permute-start(bf16[880,128]{1,0:T(8,128)(2,1)S(1)} %get-tuple-element.69), channel_id=1, source_target_pairs={{0,32},{32,0},{1,33},{33,1},{2,34},{34,2},{3,35},{35,3},{4,36},{36... | collective-permute-start | bytes 675848 | tf_op jit(solution)/shard_map/ppermute | solution.py:515
  70.2 8.4 %collective-permute-start.6 = (bf16[880,128]{1,0:T(8,128)(2,1)S(1)}, bf16[880,128]{1,0:T(8,128)(2,1)S(1)}, u32[]{:S(2)}, u32[]{:S(2)}) collective-permute-start(bf16[880,128]{1,0:T(8,128)(2,1)S(1)} %add.7), channel_id=1, source_target_pairs={{0,64},{64,0},{128,192},{192,128},{1,65},{65,1},{129,193},{193,129... | collective-permute-start | bytes 675848 | tf_op jit(solution)/shard_map/ppermute | solution.py:511
  70.8 19.6 %collective-permute-start.4 = (bf16[880,128]{1,0:T(8,128)(2,1)S(1)}, bf16[880,128]{1,0:T(8,128)(2,1)S(1)}, u32[]{:S(2)}, u32[]{:S(2)}) collective-permute-start(bf16[880,128]{1,0:T(8,128)(2,1)S(1)} %add.8), channel_id=1, source_target_pairs={{0,64},{64,0},{128,192},{192,128},{1,65},{65,1},{129,193},{193,129... | collective-permute-start | bytes 675848 | tf_op jit(solution)/shard_map/ppermute | solution.py:511
  72.3 18.2 %collective-permute-start.3 = (bf16[880,128]{1,0:T(8,128)(2,1)S(1)}, bf16[880,128]{1,0:T(8,128)(2,1)S(1)}, u32[]{:S(2)}, u32[]{:S(2)}) collective-permute-start(bf16[880,128]{1,0:T(8,128)(2,1)S(1)} %get-tuple-element.65), channel_id=1, source_target_pairs={{0,32},{32,0},{1,33},{33,1},{2,34},{34,2},{3,35},{35,3},{4,36},{36... | collective-permute-start | bytes 675848 | tf_op jit(solution)/shard_map/ppermute | solution.py:515
  78.7 11.7 %collective-permute-start.7 = (bf16[880,128]{1,0:T(8,128)(2,1)S(1)}, bf16[880,128]{1,0:T(8,128)(2,1)S(1)}, u32[]{:S(2)}, u32[]{:S(2)}) collective-permute-start(bf16[880,128]{1,0:T(8,128)(2,1)S(1)} %add.9), channel_id=1, source_target_pairs={{0,128},{64,192},{128,0},{192,64},{1,129},{65,193},{129,1},{193,65... | collective-permute-start | bytes 675848 | tf_op jit(solution)/shard_map/ppermute | solution.py:511
  90.6 6.3 %collective-permute-start.10 = (bf16[48,1152]{1,0:T(8,128)(2,1)S(1)}, bf16[48,1152]{1,0:T(8,128)(2,1)S(1)}, u32[]{:S(2)}, u32[]{:S(2)}) collective-permute-start(bf16[48,1152]{1,0:T(8,128)(2,1)S(1)} %activate.1.refs_0_), channel_id=1, source_target_pairs={{0,128},{64,192},{128,0},{192,64},{1,129},{65,193},{129,1},{193,65... | collective-permute-start | bytes 331784 | tf_op jit(solution)/shard_map/ppermute | solution.py:511
  90.7 6.2 %collective-permute-start.9 = (bf16[48,1152]{1,0:T(8,128)(2,1)S(1)}, bf16[48,1152]{1,0:T(8,128)(2,1)S(1)}, u32[]{:S(2)}, u32[]{:S(2)}) collective-permute-start(bf16[48,1152]{1,0:T(8,128)(2,1)S(1)} %activate.1.refs_0_), channel_id=1, source_target_pairs={{0,64},{64,0},{128,192},{192,128},{1,65},{65,1},{129,193},{193,129... | collective-permute-start | bytes 331784 | tf_op jit(solution)/shard_map/ppermute | solution.py:511
  93.0 1.2 collective-permute-start.11
  96.9 4.7 %collective-permute-start.12 = (bf16[48,1152]{1,0:T(8,128)(2,1)S(1)}, bf16[48,1152]{1,0:T(8,128)(2,1)S(1)}, u32[]{:S(2)}, u32[]{:S(2)}) collective-permute-start(bf16[48,1152]{1,0:T(8,128)(2,1)S(1)} %collective-permute-done.10.refs_2_), channel_id=1, source_target_pairs={{0,64},{64,0},{128,192},{192,128},{1,65},{65,1},{129,193},{193,129... | collective-permute-start | bytes 331784 | tf_op jit(solution)/shard_map/ppermute | solution.py:511
  117.5 4.5 %collective-permute-start.13 = (bf16[8,896]{1,0:T(8,128)(2,1)S(1)}, bf16[8,896]{1,0:T(8,128)(2,1)S(1)}, u32[]{:S(2)}, u32[]{:S(2)}) collective-permute-start(bf16[8,896]{1,0:T(8,128)(2,1)S(1)} %get-tuple-element.86), channel_id=1, source_target_pairs={{0,64},{64,0},{128,192},{192,128},{1,65},{65,1},{129,193},{193,129... | collective-permute-start | bytes 43016 | tf_op jit(solution)/shard_map/ppermute | solution.py:511
  117.6 4.7 %collective-permute-start.14 = (bf16[8,896]{1,0:T(8,128)(2,1)S(1)}, bf16[8,896]{1,0:T(8,128)(2,1)S(1)}, u32[]{:S(2)}, u32[]{:S(2)}) collective-permute-start(bf16[8,896]{1,0:T(8,128)(2,1)S(1)} %get-tuple-element.87), channel_id=1, source_target_pairs={{0,128},{64,192},{128,0},{192,64},{1,129},{65,193},{129,1},{193,65... | collective-permute-start | bytes 43016 | tf_op jit(solution)/shard_map/ppermute | solution.py:511
  119.8 5.5 %collective-permute-start.15 = (bf16[8,896]{1,0:T(8,128)(2,1)S(1)}, bf16[8,896]{1,0:T(8,128)(2,1)S(1)}, u32[]{:S(2)}, u32[]{:S(2)}) collective-permute-start(bf16[8,896]{1,0:T(8,128)(2,1)S(1)} %get-tuple-element.88), channel_id=1, source_target_pairs={{0,192},{64,128},{128,64},{192,0},{1,193},{65,129},{129,65},{193,1... | collective-permute-start | bytes 43016 | tf_op jit(solution)/shard_map/ppermute | solution.py:511

commit v3 on v2

--- a/solution.py
+++ b/solution.py
@@ -135,21 +135,6 @@
     )(slots, lengths, queries, key_cache, value_cache)
 
 
-def spread_shares(order, own, other, source):
-    z_count, _, ffn_count, micro = order
-    count = own.shape[0]
-
-    def place_of(r):
-        m = r % micro
-        z = (r // micro) % z_count
-        share = (r // (micro * z_count)) % 2
-        f = r // (micro * z_count * 2)
-        return share * count + source(z, f, m)
-
-    spread = one_hot((2 * count, 2 * count), place_of).astype(BF16)
-    return jnp.dot(spread, jnp.concatenate([own, other], axis=0), preferred_element_type=F32).astype(BF16)
-
-
 def rows_kernel(pieces, in_ref, out_ref, wide):
     rows, tile_rows, lanes = in_ref.shape
     wide[...] = in_ref[...].astype(F32).reshape(rows * tile_rows, lanes)
@@ -219,46 +204,59 @@
     )(core, own, rows, weight)
 
 
-def down_most_kernel(*refs):
-    *piece_refs, own_ref, other_ref, own_out_ref, other_out_ref = refs
+def placed_rows(order, me, hops, rows, own_ref, other_ref):
+    z_count, _, ffn_count, micro = order
+    count = rows.shape[0]
+    shares = [
+        jnp.dot(rows, ref[...], preferred_element_type=F32).astype(BF16) for ref in (own_ref, other_ref)
+    ]
+
+    def source(r):
+        m = r % micro
+        hop = ((r // micro) % z_count) ^ me
+        share = (r // (micro * z_count)) % 2
+        f = r // (micro * z_count * 2)
+        at = share * count + ((hop - hops[0]) * ffn_count + f) * micro + m
+        return jnp.where(jnp.logical_and(hop >= hops[0], hop <= hops[-1]), at, -1)
+
+    spread = one_hot((2 * z_count * ffn_count * micro, 2 * count), source).astype(BF16)
+    return jnp.dot(spread, jnp.concatenate(shares, axis=0), preferred_element_type=F32)
+
+
+def down_most_kernel(order, z_ref, *refs):
+    *piece_refs, own_ref, other_ref, out_ref = refs
     rows = jnp.concatenate([ref[...] for ref in piece_refs], axis=0)
-    own_out_ref[...] = jnp.dot(rows, own_ref[...], preferred_element_type=F32).astype(BF16)
-    other_out_ref[...] = jnp.dot(rows, other_ref[...], preferred_element_type=F32).astype(BF16)
-
-
-def down_most(pieces, own_weight, other_weight):
-    shape = jax.ShapeDtypeStruct((len(pieces) * pieces[0].shape[0], own_weight.shape[1]), BF16)
-    return pl.pallas_call(
-        down_most_kernel,
-        out_shape=(shape, shape),
-        in_specs=[whole()] * (len(pieces) + 2),
-        out_specs=(whole(), whole()),
+    hops = range(len(piece_refs))
+    out_ref[...] = placed_rows(order, z_ref[0], hops, rows, own_ref, other_ref).astype(BF16)
+
+
+def down_most(z, pieces, own_weight, other_weight, order):
+    z_count, _, ffn_count, micro = order
+    return pl.pallas_call(
+        functools.partial(down_most_kernel, order),
+        out_shape=jax.ShapeDtypeStruct((2 * z_count * ffn_count * micro, own_weight.shape[1]), BF16),
+        in_specs=[scalars()] + [whole()] * (len(pieces) + 2),
+        out_specs=whole(),
         compiler_params=params(16),
         cost_estimate=HEAVY,
         name="down_most",
-    )(*pieces, own_weight, other_weight)
-
-
-def down_kernel(order, z_ref, own_most_ref, other_most_ref, rows_ref, own_ref, other_ref, out_ref):
-    _, _, ffn_count, micro = order
-    shares = []
-    for most_ref, weight_ref in ((own_most_ref, own_ref), (other_most_ref, other_ref)):
-        last = jnp.dot(rows_ref[...], weight_ref[...], preferred_element_type=F32).astype(BF16)
-        shares.append(jnp.concatenate([most_ref[...], last], axis=0))
-    me = z_ref[0]
-    out_ref[...] = spread_shares(order, *shares, lambda z, f, m: ((z ^ me) * ffn_count + f) * micro + m)
+    )(z, *pieces, own_weight, other_weight)
+
+
+def down_kernel(order, z_ref, most_ref, rows_ref, own_ref, other_ref, out_ref):
+    last = placed_rows(order, z_ref[0], (order[0] - 1,), rows_ref[...], own_ref, other_ref)
+    out_ref[...] = (most_ref[...].astype(F32) + last).astype(BF16)
 
 
 def down(z, most, last, own_weight, other_weight, order):
-    rows = most[0].shape[0] + last.shape[0]
     return pl.pallas_call(
         functools.partial(down_kernel, order),
-        out_shape=jax.ShapeDtypeStruct((2 * rows, own_weight.shape[1]), BF16),
-        in_specs=[scalars()] + [whole()] * 5,
+        out_shape=jax.ShapeDtypeStruct(most.shape, BF16),
+        in_specs=[scalars()] + [whole()] * 4,
         out_specs=whole(),
         compiler_params=params(16),
         name="down",
-    )(z, *most, last, own_weight, other_weight)
+    )(z, most, last, own_weight, other_weight)
 
 
 def fetch_kernel(cuts, *refs):
@@ -586,7 +584,7 @@
     far = along_z(activated, 2)
     near = along_z(activated, 1)
     far, received = lax.optimization_barrier((far, swap_cores(send)))
-    most = down_most((activated, near, far), down_own, down_other)
+    most = down_most(z_index, (activated, near, far), down_own, down_other, order)
     lowered = down(z_index, most, along_z(far, 1), down_own, down_other, order)
     lowered_parts = lax.all_to_all(
         lowered.reshape(ffn_count, rows_chunk, col_share), FFN, split_axis=0, concat_axis=0, tiled=True

time: 126 us -> 126 us (level)
  transfers between devices with their start and end apart: 16 -> 16, of which waited for: 9 -> 9; matrix products, arithmetic and copies ran while one was open for 0% -> 0% of each run, Pallas kernels for 5% -> 6%
where the time goes in v3:
time: 126 us
  blocking collectives  72.9 us (58%)
  waiting for transfers between devices  25.5 us (20%)
  Pallas kernels  16 us (13%)
  starting transfers between devices  11.1 us (9%)
    all_to_all x1, blocking collectives, per_device(): lax.all_to_all(payload, (Z,) + FFN, split_axis=0, concat_axis=0, tiled=True)  26.3 us
    ppermute x9, waiting for transfers between devices, along_z(): lax.ppermute(array, Z, [(i, i ^ hop) for i in range(lax.axis_size(Z))])  21.9 us
    all_to_all x1, blocking collectives, per_device(): lax.all_to_all(mixed.reshape(ffn_count, rows_chunk, col_share), FFN, spli...  16.8 us
    all_to_all x1, blocking collectives, per_device(): lax.all_to_all(copies, FFN, split_axis=0, concat_axis=0, tiled=True)  15.6 us
    all_to_all x1, blocking collectives, per_device(): lax.all_to_all(lowered.reshape(ffn_count, rows_chunk, col_share), FFN, sp...  14.2 us
    ppermute x9, starting transfers between devices, along_z(): lax.ppermute(array, Z, [(i, i ^ hop) for i in range(lax.axis_size(Z))])  9.73 us
    pallas_call x1, Pallas kernels, attend(): pl.pallas_call(attention_kernel, in_specs=[in_hbm()] * 5, out_specs=whole...  3.67 us
    ppermute x7, waiting for transfers between devices, swap_cores(): return lax.ppermute(array, CORE, [(0, 1), (1, 0)])  3.64 us
  transfers between devices with their start and end apart: 16, of which 9 were waited for; matrix products, arithmetic and copies ran while one was open for 0% of the time, Pallas kernels for 6%

profile of v3, /device:TPU:8, one launch (start us, length us, event | category | flops | bytes accessed | tf_op | source)
XLA Modules:
  0.0 125.8 jit_solution(351024253060424415)
XLA Ops:
  0.0 3.7 %attention.1 = bf16[4,16,3,8,128]{4,3,2,1,0:T(8,128)(2,1)} custom-call(s32[1,3]{1,0:T(1,128)} %bitcast.21, s32[1,3]{1,0:T(1,128)} %bitcast.22, bf16[3,16384]{1,0:T(4,128)(2,1)} %bitcast.20, bf16[3,1024,256]{2,1,0:T(8,128)(2,1)} %key_hbm.1, bf16[3,1024,256]{2,1,0:T(8,128)(2,1)} %value_hbm.1), custom_call_target="tpu_custom_call" | custom-call | tf_op jit(solution)/shard_map/attention/pallas_call | solution.py:117
  3.7 26.3 %all_to_all.20 = bf16[64,24,128]{2,1,0:T(8,128)(2,1)S(1)} all-to-all(bf16[64,24,128]{2,1,0:T(8,128)(2,1)} %bitcast.19), channel_id=1, replica_groups=mesh['z'=4,'core'=2,'x'=4,'y'=4,'rep'=2] {'z','x','y'}, dimensions={0} | all-to-all | bytes 786432 | tf_op jit(solution)/shard_map/all_to_all | solution.py:551
  30.3 1.0 product.1.own_ref
  32.0 1.0 mix.1
  33.0 16.8 %all_to_all.21.parts_ref = bf16[16,24,896]{2,1,0:T(8,128)(2,1)S(1)} all-to-all(bf16[16,24,896]{2,1,0:T(8,128)(2,1)S(1)} %bitcast.14), channel_id=1, replica_groups=mesh['z'=4,'core'=2,'x'=4,'y'=4,'rep'=2] {'x','y'}, dimensions={0} | all-to-all | bytes 1376256 | tf_op jit(solution)/shard_map/all_to_all | solution.py:560
  50.2 15.6 %all_to_all.22 = bf16[16,24,896]{2,1,0:T(8,128)(2,1)S(1)} all-to-all(bf16[16,24,896]{2,1,0:T(8,128)(2,1)S(1)} %get-tuple-element.53), channel_id=1, replica_groups=mesh['z'=4,'core'=2,'x'=4,'y'=4,'rep'=2] {'x','y'}, dimensions={0} | all-to-all | bytes 1376256 | tf_op jit(solution)/shard_map/all_to_all | solution.py:564
  65.8 1.5 %up_part.2 = (bf16[880,128]{1,0:T(8,128)(2,1)S(1)}, bf16[880,128]{1,0:T(8,128)(2,1)S(1)}, bf16[880,128]{1,0:T(8,128)(2,1)S(1)}, bf16[880,128]{1,0:T(8,128)(2,1)S(1)}) custom-call(s32[1]{0:T(128)} %bitcast.4.z_ref, s32[1]{0:T(128)} %bitcast.5.core_ref, bf16[384,896]{1,0:T(8,128)(2,1)S(1)} %bitcast.17, bf16[1,896]{1,0:T(2,128)(2,1)S(1)} %broadcast_in_dim.15.gain_ref, ...), custom_call_target="tpu_custom_call" | custom-call | flops 10000000000 | bytes 10000000 | tf_op jit(solution)/shard_map/up_part/pallas_call | solution.py:379
  67.9 1.5 %up_part.3 = (bf16[880,128]{1,0:T(8,128)(2,1)S(1)}, bf16[880,128]{1,0:T(8,128)(2,1)S(1)}, bf16[880,128]{1,0:T(8,128)(2,1)S(1)}, bf16[880,128]{1,0:T(8,128)(2,1)S(1)}) custom-call(s32[1]{0:T(128)} %bitcast.4.z_ref, s32[1]{0:T(128)} %bitcast.5.core_ref, bf16[384,896]{1,0:T(8,128)(2,1)S(1)} %bitcast.18, bf16[1,896]{1,0:T(2,128)(2,1)S(1)} %broadcast_in_dim.15.gain_ref, ...), custom_call_target="tpu_custom_call" | custom-call | flops 10000000000 | bytes 10000000 | tf_op jit(solution)/shard_map/up_part/pallas_call | solution.py:379
  70.8 1.4 %collective-permute-start.4 = (bf16[880,128]{1,0:T(8,128)(2,1)S(1)}, bf16[880,128]{1,0:T(8,128)(2,1)S(1)}, u32[]{:S(2)}, u32[]{:S(2)}) collective-permute-start(bf16[880,128]{1,0:T(8,128)(2,1)S(1)} %add.8), channel_id=1, source_target_pairs={{0,64},{64,0},{128,192},{192,128},{1,65},{65,1},{129,193},{193,129... | collective-permute-start | bytes 675848 | tf_op jit(solution)/shard_map/ppermute | solution.py:509
  72.3 1.7 %collective-permute-done.5.refs_1_ = bf16[880,128]{1,0:T(8,128)(2,1)S(1)} collective-permute-done((bf16[880,128]{1,0:T(8,128)(2,1)S(1)}, bf16[880,128]{1,0:T(8,128)(2,1)S(1)}, u32[]{:S(2)}, u32[]{:S(2)}) %collective-permute-start.5) | collective-permute-done | bytes 225312 | tf_op jit(solution)/shard_map/ppermute | solution.py:513
  74.0 4.6 %collective-permute-done.6.refs_2_ = bf16[880,128]{1,0:T(8,128)(2,1)S(1)} collective-permute-done((bf16[880,128]{1,0:T(8,128)(2,1)S(1)}, bf16[880,128]{1,0:T(8,128)(2,1)S(1)}, u32[]{:S(2)}, u32[]{:S(2)}) %collective-permute-start.6) | collective-permute-done | bytes 225312 | tf_op jit(solution)/shard_map/ppermute | solution.py:509
  78.7 1.0 collective-permute-start.7
  79.7 2.8 %fetch.1 = (bf16[1152,896]{1,0:T(8,128)(2,1)S(1)}, bf16[1152,896]{1,0:T(8,128)(2,1)S(1)}) custom-call(bf16[1152,896]{1,0:T(8,128)(2,1)S(1)} %copy-done.4, bf16[1152,896]{1,0:T(8,128)(2,1)S(1)} %collective-permute-done.8.refs_1_), custom_call_target="tpu_custom_call" | custom-call | flops 10000000000 | bytes 10000000 | tf_op jit(solution)/shard_map/fetch/pallas_call | solution.py:279
  82.5 7.9 %collective-permute-done.7.refs_3_ = bf16[880,128]{1,0:T(8,128)(2,1)S(1)} collective-permute-done((bf16[880,128]{1,0:T(8,128)(2,1)S(1)}, bf16[880,128]{1,0:T(8,128)(2,1)S(1)}, u32[]{:S(2)}, u32[]{:S(2)}) %collective-permute-start.7) | collective-permute-done | bytes 225312 | tf_op jit(solution)/shard_map/ppermute | solution.py:509
  90.8 2.2 %collective-permute-start.9 = (bf16[48,1152]{1,0:T(8,128)(2,1)S(1)}, bf16[48,1152]{1,0:T(8,128)(2,1)S(1)}, u32[]{:S(2)}, u32[]{:S(2)}) collective-permute-start(bf16[48,1152]{1,0:T(8,128)(2,1)S(1)} %activate.1.refs_0_), channel_id=1, source_target_pairs={{0,64},{64,0},{128,192},{192,128},{1,65},{65,1},{129,193},{193,129... | collective-permute-start | bytes 331784 | tf_op jit(solution)/shard_map/ppermute | solution.py:509
  92.9 1.2 collective-permute-done.11.received_ref
  94.1 2.8 %collective-permute-done.10.refs_2_ = bf16[48,1152]{1,0:T(8,128)(2,1)S(1)} collective-permute-done((bf16[48,1152]{1,0:T(8,128)(2,1)S(1)}, bf16[48,1152]{1,0:T(8,128)(2,1)S(1)}, u32[]{:S(2)}, u32[]{:S(2)}) %collective-permute-start.10) | collective-permute-done | bytes 110624 | tf_op jit(solution)/shard_map/ppermute | solution.py:509
  96.9 1.5 %down_most.1.most_ref = bf16[384,896]{1,0:T(8,128)(2,1)S(1)} custom-call(s32[1]{0:T(128)} %bitcast.4.z_ref, bf16[48,1152]{1,0:T(8,128)(2,1)S(1)} %activate.1.refs_0_, bf16[48,1152]{1,0:T(8,128)(2,1)S(1)} %collective-permute-done.9.refs_1_, bf16[48,1152]{1,0:T(8,128)(2,1)S(1)} %collective-permute-done.10.refs_2_, ...), custom_call_target="tpu_custom_call" | custom-call | flops 10000000000 | bytes 10000000 | tf_op jit(solution)/shard_map/down_most/pallas_call | solution.py:235
  98.5 3.2 %collective-permute-done.12.rows_ref = bf16[48,1152]{1,0:T(8,128)(2,1)S(1)} collective-permute-done((bf16[48,1152]{1,0:T(8,128)(2,1)S(1)}, bf16[48,1152]{1,0:T(8,128)(2,1)S(1)}, u32[]{:S(2)}, u32[]{:S(2)}) %collective-permute-start.12) | collective-permute-done | bytes 110624 | tf_op jit(solution)/shard_map/ppermute | solution.py:509
  101.7 1.1 down.1
  102.8 14.2 %all_to_all.23.parts_ref = bf16[16,24,896]{2,1,0:T(8,128)(2,1)S(1)} all-to-all(bf16[16,24,896]{2,1,0:T(8,128)(2,1)S(1)} %bitcast.13), channel_id=1, replica_groups=mesh['z'=4,'core'=2,'x'=4,'y'=4,'rep'=2] {'x','y'}, dimensions={0} | all-to-all | bytes 1376256 | tf_op jit(solution)/shard_map/all_to_all | solution.py:589
  117.4 2.2 %collective-permute-start.14 = (bf16[8,896]{1,0:T(8,128)(2,1)S(1)}, bf16[8,896]{1,0:T(8,128)(2,1)S(1)}, u32[]{:S(2)}, u32[]{:S(2)}) collective-permute-start(bf16[8,896]{1,0:T(8,128)(2,1)S(1)} %get-tuple-element.83), channel_id=1, source_target_pairs={{0,128},{64,192},{128,0},{192,64},{1,129},{65,193},{129,1},{193,65... | collective-permute-start | bytes 43016 | tf_op jit(solution)/shard_map/ppermute | solution.py:509
  119.6 2.1 %collective-permute-start.15 = (bf16[8,896]{1,0:T(8,128)(2,1)S(1)}, bf16[8,896]{1,0:T(8,128)(2,1)S(1)}, u32[]{:S(2)}, u32[]{:S(2)}) collective-permute-start(bf16[8,896]{1,0:T(8,128)(2,1)S(1)} %get-tuple-element.84), channel_id=1, source_target_pairs={{0,192},{64,128},{128,64},{192,0},{1,193},{65,129},{129,65},{193,1... | collective-permute-start | bytes 43016 | tf_op jit(solution)/shard_map/ppermute | solution.py:509
  122.1 3.1 %collective-permute-done.15.refs_3_ = bf16[8,896]{1,0:T(8,128)(2,1)S(1)} collective-permute-done((bf16[8,896]{1,0:T(8,128)(2,1)S(1)}, bf16[8,896]{1,0:T(8,128)(2,1)S(1)}, u32[]{:S(2)}, u32[]{:S(2)}) %collective-permute-start.15) | collective-permute-done | bytes 14368 | tf_op jit(solution)/shard_map/ppermute | solution.py:509
  (41 shorter events, 5.1 us)
Async XLA Ops:
  0.0 30.3 %copy-start = (bf16[1024,896]{1,0:T(8,128)(2,1)S(1)}, bf16[1024,896]{1,0:T(8,128)(2,1)}, u32[]{:S(2)}) copy-start(bf16[1024,896]{1,0:T(8,128)(2,1)} %weight_ref.3) | copy-start | bytes 5505028
  30.2 1.1 copy-start.5
  30.2 1.8 %collective-permute-start = (bf16[192,1024]{1,0:T(8,128)(2,1)S(1)}, bf16[192,1024]{1,0:T(8,128)(2,1)S(1)}, u32[]{:S(2)}, u32[]{:S(2)}) collective-permute-start(bf16[192,1024]{1,0:T(8,128)(2,1)S(1)} %to_rows.1.rows_ref), channel_id=1, source_target_pairs={{0,32},{32,0},{1,33},{33,1},{2,34},{34,2},{3,35},{35,3},{4,36},{36... | collective-permute-start | bytes 1179656 | tf_op jit(solution)/shard_map/ppermute | solution.py:513
  31.3 18.5 %copy-start.1 = (bf16[3,128,896]{2,1,0:T(8,128)(2,1)S(1)}, bf16[3,128,896]{2,1,0:T(8,128)(2,1)}, u32[]{:S(2)}) copy-start(bf16[3,128,896]{2,1,0:T(8,128)(2,1)} %param.11) | copy-start | bytes 2064388
  33.0 32.8 %copy-start.2 = (bf16[896,1152]{1,0:T(8,128)(2,1)S(1)}, bf16[896,1152]{1,0:T(8,128)(2,1)}, u32[]{:S(2)}) copy-start(bf16[896,1152]{1,0:T(8,128)(2,1)} %gate_ref.3) | copy-start | bytes 6193156
  33.0 32.8 %copy-start.3 = (bf16[896,1152]{1,0:T(8,128)(2,1)S(1)}, bf16[896,1152]{1,0:T(8,128)(2,1)}, u32[]{:S(2)}) copy-start(bf16[896,1152]{1,0:T(8,128)(2,1)} %up_ref.3) | copy-start | bytes 6193156
  67.3 2.1 %collective-permute-start.1 = (bf16[880,128]{1,0:T(8,128)(2,1)S(1)}, bf16[880,128]{1,0:T(8,128)(2,1)S(1)}, u32[]{:S(2)}, u32[]{:S(2)}) collective-permute-start(bf16[880,128]{1,0:T(8,128)(2,1)S(1)} %get-tuple-element.55), channel_id=1, source_target_pairs={{0,32},{32,0},{1,33},{33,1},{2,34},{34,2},{3,35},{35,3},{4,36},{36... | collective-permute-start | bytes 675848 | tf_op jit(solution)/shard_map/ppermute | solution.py:513
  67.4 2.1 %copy-start.4 = (bf16[1152,896]{1,0:T(8,128)(2,1)S(1)}, bf16[1152,896]{1,0:T(8,128)(2,1)}, u32[]{:S(2)}) copy-start(bf16[1152,896]{1,0:T(8,128)(2,1)} %refs_0_) | copy-start | bytes 6193156
  67.4 2.0 %collective-permute-start.2 = (bf16[880,128]{1,0:T(8,128)(2,1)S(1)}, bf16[880,128]{1,0:T(8,128)(2,1)S(1)}, u32[]{:S(2)}, u32[]{:S(2)}) collective-permute-start(bf16[880,128]{1,0:T(8,128)(2,1)S(1)} %get-tuple-element.56), channel_id=1, source_target_pairs={{0,32},{32,0},{1,33},{33,1},{2,34},{34,2},{3,35},{35,3},{4,36},{36... | collective-permute-start | bytes 675848 | tf_op jit(solution)/shard_map/ppermute | solution.py:513
  69.5 10.2 %collective-permute-start.8 = (bf16[1152,896]{1,0:T(8,128)(2,1)S(1)}, bf16[1152,896]{1,0:T(8,128)(2,1)S(1)}, u32[]{:S(2)}, u32[]{:S(2)}) collective-permute-start(bf16[1152,896]{1,0:T(8,128)(2,1)S(1)} %copy-done.4), channel_id=1, source_target_pairs={{0,32},{32,0},{1,33},{33,1},{2,34},{34,2},{3,35},{35,3},{4,36},{36... | collective-permute-start | bytes 6193160 | tf_op jit(solution)/shard_map/ppermute | solution.py:513
  69.8 4.3 %collective-permute-start.5 = (bf16[880,128]{1,0:T(8,128)(2,1)S(1)}, bf16[880,128]{1,0:T(8,128)(2,1)S(1)}, u32[]{:S(2)}, u32[]{:S(2)}) collective-permute-start(bf16[880,128]{1,0:T(8,128)(2,1)S(1)} %get-tuple-element.67), channel_id=1, source_target_pairs={{0,32},{32,0},{1,33},{33,1},{2,34},{34,2},{3,35},{35,3},{4,36},{36... | collective-permute-start | bytes 675848 | tf_op jit(solution)/shard_map/ppermute | solution.py:513
  70.3 8.4 %collective-permute-start.6 = (bf16[880,128]{1,0:T(8,128)(2,1)S(1)}, bf16[880,128]{1,0:T(8,128)(2,1)S(1)}, u32[]{:S(2)}, u32[]{:S(2)}) collective-permute-start(bf16[880,128]{1,0:T(8,128)(2,1)S(1)} %add.7), channel_id=1, source_target_pairs={{0,64},{64,0},{128,192},{192,128},{1,65},{65,1},{129,193},{193,129... | collective-permute-start | bytes 675848 | tf_op jit(solution)/shard_map/ppermute | solution.py:509
  70.8 19.6 %collective-permute-start.4 = (bf16[880,128]{1,0:T(8,128)(2,1)S(1)}, bf16[880,128]{1,0:T(8,128)(2,1)S(1)}, u32[]{:S(2)}, u32[]{:S(2)}) collective-permute-start(bf16[880,128]{1,0:T(8,128)(2,1)S(1)} %add.8), channel_id=1, source_target_pairs={{0,64},{64,0},{128,192},{192,128},{1,65},{65,1},{129,193},{193,129... | collective-permute-start | bytes 675848 | tf_op jit(solution)/shard_map/ppermute | solution.py:509
  72.3 18.2 %collective-permute-start.3 = (bf16[880,128]{1,0:T(8,128)(2,1)S(1)}, bf16[880,128]{1,0:T(8,128)(2,1)S(1)}, u32[]{:S(2)}, u32[]{:S(2)}) collective-permute-start(bf16[880,128]{1,0:T(8,128)(2,1)S(1)} %get-tuple-element.63), channel_id=1, source_target_pairs={{0,32},{32,0},{1,33},{33,1},{2,34},{34,2},{3,35},{35,3},{4,36},{36... | collective-permute-start | bytes 675848 | tf_op jit(solution)/shard_map/ppermute | solution.py:513
  78.7 11.7 %collective-permute-start.7 = (bf16[880,128]{1,0:T(8,128)(2,1)S(1)}, bf16[880,128]{1,0:T(8,128)(2,1)S(1)}, u32[]{:S(2)}, u32[]{:S(2)}) collective-permute-start(bf16[880,128]{1,0:T(8,128)(2,1)S(1)} %add.9), channel_id=1, source_target_pairs={{0,128},{64,192},{128,0},{192,64},{1,129},{65,193},{129,1},{193,65... | collective-permute-start | bytes 675848 | tf_op jit(solution)/shard_map/ppermute | solution.py:509
  90.7 6.3 %collective-permute-start.10 = (bf16[48,1152]{1,0:T(8,128)(2,1)S(1)}, bf16[48,1152]{1,0:T(8,128)(2,1)S(1)}, u32[]{:S(2)}, u32[]{:S(2)}) collective-permute-start(bf16[48,1152]{1,0:T(8,128)(2,1)S(1)} %activate.1.refs_0_), channel_id=1, source_target_pairs={{0,128},{64,192},{128,0},{192,64},{1,129},{65,193},{129,1},{193,65... | collective-permute-start | bytes 331784 | tf_op jit(solution)/shard_map/ppermute | solution.py:509
  90.8 6.2 %collective-permute-start.9 = (bf16[48,1152]{1,0:T(8,128)(2,1)S(1)}, bf16[48,1152]{1,0:T(8,128)(2,1)S(1)}, u32[]{:S(2)}, u32[]{:S(2)}) collective-permute-start(bf16[48,1152]{1,0:T(8,128)(2,1)S(1)} %activate.1.refs_0_), channel_id=1, source_target_pairs={{0,64},{64,0},{128,192},{192,128},{1,65},{65,1},{129,193},{193,129... | collective-permute-start | bytes 331784 | tf_op jit(solution)/shard_map/ppermute | solution.py:509
  92.9 1.2 collective-permute-start.11
  96.9 4.7 %collective-permute-start.12 = (bf16[48,1152]{1,0:T(8,128)(2,1)S(1)}, bf16[48,1152]{1,0:T(8,128)(2,1)S(1)}, u32[]{:S(2)}, u32[]{:S(2)}) collective-permute-start(bf16[48,1152]{1,0:T(8,128)(2,1)S(1)} %collective-permute-done.10.refs_2_), channel_id=1, source_target_pairs={{0,64},{64,0},{128,192},{192,128},{1,65},{65,1},{129,193},{193,129... | collective-permute-start | bytes 331784 | tf_op jit(solution)/shard_map/ppermute | solution.py:509
  117.3 4.5 %collective-permute-start.13 = (bf16[8,896]{1,0:T(8,128)(2,1)S(1)}, bf16[8,896]{1,0:T(8,128)(2,1)S(1)}, u32[]{:S(2)}, u32[]{:S(2)}) collective-permute-start(bf16[8,896]{1,0:T(8,128)(2,1)S(1)} %get-tuple-element.82), channel_id=1, source_target_pairs={{0,64},{64,0},{128,192},{192,128},{1,65},{65,1},{129,193},{193,129... | collective-permute-start | bytes 43016 | tf_op jit(solution)/shard_map/ppermute | solution.py:509
  117.4 4.7 %collective-permute-start.14 = (bf16[8,896]{1,0:T(8,128)(2,1)S(1)}, bf16[8,896]{1,0:T(8,128)(2,1)S(1)}, u32[]{:S(2)}, u32[]{:S(2)}) collective-permute-start(bf16[8,896]{1,0:T(8,128)(2,1)S(1)} %get-tuple-element.83), channel_id=1, source_target_pairs={{0,128},{64,192},{128,0},{192,64},{1,129},{65,193},{129,1},{193,65... | collective-permute-start | bytes 43016 | tf_op jit(solution)/shard_map/ppermute | solution.py:509
  119.6 5.5 %collective-permute-start.15 = (bf16[8,896]{1,0:T(8,128)(2,1)S(1)}, bf16[8,896]{1,0:T(8,128)(2,1)S(1)}, u32[]{:S(2)}, u32[]{:S(2)}) collective-permute-start(bf16[8,896]{1,0:T(8,128)(2,1)S(1)} %get-tuple-element.84), channel_id=1, source_target_pairs={{0,192},{64,128},{128,64},{192,0},{1,193},{65,129},{129,65},{193,1... | collective-permute-start | bytes 43016 | tf_op jit(solution)/shard_map/ppermute | solution.py:509

commit v4 on v3

--- a/solution.py
+++ b/solution.py
@@ -567,13 +567,15 @@
     up_args = (z_index, core_index, stream_all, gain, gate_weight, up_weight)
     own3, own1, other3, other1 = up_part(order, (3, 1), *up_args)
     own0, own2, other0, other2 = up_part(order, (0, 2), *up_args)
-    received3, received1, own0 = lax.optimization_barrier((swap_cores(other3), swap_cores(other1), own0))
+    own3, send = lax.optimization_barrier((own3, send))
+    received3, received1, own0, received = lax.optimization_barrier(
+        (swap_cores(other3), swap_cores(other1), own0, swap_cores(send))
+    )
     relayed3 = add(own3, received3)
     near1 = add(own1, received1)
     relayed3, other0, other2 = lax.optimization_barrier((relayed3, other0, other2))
     crossing = along_z(relayed3, 1)
     relayed = add(own2, swap_cores(other2), crossing)
-    relayed, send = lax.optimization_barrier((relayed, send))
     from_far = along_z(relayed, 2)
     from_near = along_z(near1, 1)
     down_weight, near1 = lax.optimization_barrier((down_weight, near1))
@@ -583,7 +585,6 @@
 
     far = along_z(activated, 2)
     near = along_z(activated, 1)
-    far, received = lax.optimization_barrier((far, swap_cores(send)))
     most = down_most(z_index, (activated, near, far), down_own, down_other, order)
     lowered = down(z_index, most, along_z(far, 1), down_own, down_other, order)
     lowered_parts = lax.all_to_all(

time: 126 us -> 127 us (level)
  waiting for transfers between devices: 25.5 us -> 26.8 us
    ppermute x9, waiting for transfers between devices: 21.9 us -> 24.3 us  [along_z(): lax.ppermute(array, Z, [(i, i ^ hop) for i in range(lax.axis_size(Z))])]
where the time goes in v4:
time: 127 us
  blocking collectives  72.9 us (57%)
  waiting for transfers between devices  26.8 us (21%)
  Pallas kernels  16 us (13%)
  starting transfers between devices  10.8 us (9%)
    all_to_all x1, blocking collectives, per_device(): lax.all_to_all(payload, (Z,) + FFN, split_axis=0, concat_axis=0, tiled=True)  26.3 us
    ppermute x9, waiting for transfers between devices, along_z(): lax.ppermute(array, Z, [(i, i ^ hop) for i in range(lax.axis_size(Z))])  24.3 us
    all_to_all x1, blocking collectives, per_device(): lax.all_to_all(mixed.reshape(ffn_count, rows_chunk, col_share), FFN, spli...  16.8 us
    all_to_all x1, blocking collectives, per_device(): lax.all_to_all(copies, FFN, split_axis=0, concat_axis=0, tiled=True)  15.6 us
    all_to_all x1, blocking collectives, per_device(): lax.all_to_all(lowered.reshape(ffn_count, rows_chunk, col_share), FFN, sp...  14.2 us
    ppermute x9, starting transfers between devices, along_z(): lax.ppermute(array, Z, [(i, i ^ hop) for i in range(lax.axis_size(Z))])  9.32 us
    pallas_call x1, Pallas kernels, attend(): pl.pallas_call(attention_kernel, in_specs=[in_hbm()] * 5, out_specs=whole...  3.67 us
    pallas_call x2, Pallas kernels, up_part(): pl.pallas_call(functools.partial(up_kernel, order, hops), out_shape=[shap...  2.99 us
  transfers between devices with their start and end apart: 16, of which 9 were waited for; matrix products, arithmetic and copies ran while one was open for 0% of the time, Pallas kernels for 6%

profile of v4, /device:TPU:8, one launch (start us, length us, event | category | flops | bytes accessed | tf_op | source)
XLA Modules:
  0.0 126.8 jit_solution(14732666171624756709)
XLA Ops:
  0.0 3.7 %attention.1 = bf16[4,16,3,8,128]{4,3,2,1,0:T(8,128)(2,1)} custom-call(s32[1,3]{1,0:T(1,128)} %bitcast.21, s32[1,3]{1,0:T(1,128)} %bitcast.22, bf16[3,16384]{1,0:T(4,128)(2,1)} %bitcast.20, bf16[3,1024,256]{2,1,0:T(8,128)(2,1)} %key_hbm.1, bf16[3,1024,256]{2,1,0:T(8,128)(2,1)} %value_hbm.1), custom_call_target="tpu_custom_call" | custom-call | tf_op jit(solution)/shard_map/attention/pallas_call | solution.py:117
  3.7 26.3 %all_to_all.20 = bf16[64,24,128]{2,1,0:T(8,128)(2,1)S(1)} all-to-all(bf16[64,24,128]{2,1,0:T(8,128)(2,1)} %bitcast.19), channel_id=1, replica_groups=mesh['z'=4,'core'=2,'x'=4,'y'=4,'rep'=2] {'z','x','y'}, dimensions={0} | all-to-all | bytes 786432 | tf_op jit(solution)/shard_map/all_to_all | solution.py:551
  30.3 1.0 product.1.own_ref
  31.3 0.7 collective-permute-done.rows_ref
  32.0 1.0 mix.1
  33.0 16.8 %all_to_all.21.parts_ref = bf16[16,24,896]{2,1,0:T(8,128)(2,1)S(1)} all-to-all(bf16[16,24,896]{2,1,0:T(8,128)(2,1)S(1)} %bitcast.14), channel_id=1, replica_groups=mesh['z'=4,'core'=2,'x'=4,'y'=4,'rep'=2] {'x','y'}, dimensions={0} | all-to-all | bytes 1376256 | tf_op jit(solution)/shard_map/all_to_all | solution.py:560
  50.2 15.6 %all_to_all.22 = bf16[16,24,896]{2,1,0:T(8,128)(2,1)S(1)} all-to-all(bf16[16,24,896]{2,1,0:T(8,128)(2,1)S(1)} %get-tuple-element.52), channel_id=1, replica_groups=mesh['z'=4,'core'=2,'x'=4,'y'=4,'rep'=2] {'x','y'}, dimensions={0} | all-to-all | bytes 1376256 | tf_op jit(solution)/shard_map/all_to_all | solution.py:564
  65.8 1.5 %up_part.2 = (bf16[880,128]{1,0:T(8,128)(2,1)S(1)}, bf16[880,128]{1,0:T(8,128)(2,1)S(1)}, bf16[880,128]{1,0:T(8,128)(2,1)S(1)}, bf16[880,128]{1,0:T(8,128)(2,1)S(1)}) custom-call(s32[1]{0:T(128)} %bitcast.4.z_ref, s32[1]{0:T(128)} %bitcast.5.core_ref, bf16[384,896]{1,0:T(8,128)(2,1)S(1)} %bitcast.17, bf16[1,896]{1,0:T(2,128)(2,1)S(1)} %broadcast_in_dim.15.gain_ref, ...), custom_call_target="tpu_custom_call" | custom-call | flops 10000000000 | bytes 10000000 | tf_op jit(solution)/shard_map/up_part/pallas_call | solution.py:379
  68.0 1.5 %up_part.3 = (bf16[880,128]{1,0:T(8,128)(2,1)S(1)}, bf16[880,128]{1,0:T(8,128)(2,1)S(1)}, bf16[880,128]{1,0:T(8,128)(2,1)S(1)}, bf16[880,128]{1,0:T(8,128)(2,1)S(1)}) custom-call(s32[1]{0:T(128)} %bitcast.4.z_ref, s32[1]{0:T(128)} %bitcast.5.core_ref, bf16[384,896]{1,0:T(8,128)(2,1)S(1)} %bitcast.18, bf16[1,896]{1,0:T(2,128)(2,1)S(1)} %broadcast_in_dim.15.gain_ref, ...), custom_call_target="tpu_custom_call" | custom-call | flops 10000000000 | bytes 10000000 | tf_op jit(solution)/shard_map/up_part/pallas_call | solution.py:379
  71.0 1.4 %collective-permute-start.5 = (bf16[880,128]{1,0:T(8,128)(2,1)S(1)}, bf16[880,128]{1,0:T(8,128)(2,1)S(1)}, u32[]{:S(2)}, u32[]{:S(2)}) collective-permute-start(bf16[880,128]{1,0:T(8,128)(2,1)S(1)} %add.8), channel_id=1, source_target_pairs={{0,64},{64,0},{128,192},{192,128},{1,65},{65,1},{129,193},{193,129... | collective-permute-start | bytes 675848 | tf_op jit(solution)/shard_map/ppermute | solution.py:509
  72.4 1.8 %collective-permute-done.6.refs_1_ = bf16[880,128]{1,0:T(8,128)(2,1)S(1)} collective-permute-done((bf16[880,128]{1,0:T(8,128)(2,1)S(1)}, bf16[880,128]{1,0:T(8,128)(2,1)S(1)}, u32[]{:S(2)}, u32[]{:S(2)}) %collective-permute-start.6) | collective-permute-done | bytes 225312 | tf_op jit(solution)/shard_map/ppermute | solution.py:513
  74.2 4.5 %collective-permute-done.7.refs_2_ = bf16[880,128]{1,0:T(8,128)(2,1)S(1)} collective-permute-done((bf16[880,128]{1,0:T(8,128)(2,1)S(1)}, bf16[880,128]{1,0:T(8,128)(2,1)S(1)}, u32[]{:S(2)}, u32[]{:S(2)}) %collective-permute-start.7) | collective-permute-done | bytes 225312 | tf_op jit(solution)/shard_map/ppermute | solution.py:509
  78.8 1.0 collective-permute-start.8
  79.8 2.8 %fetch.1 = (bf16[1152,896]{1,0:T(8,128)(2,1)S(1)}, bf16[1152,896]{1,0:T(8,128)(2,1)S(1)}) custom-call(bf16[1152,896]{1,0:T(8,128)(2,1)S(1)} %copy-done.4, bf16[1152,896]{1,0:T(8,128)(2,1)S(1)} %collective-permute-done.9.refs_1_), custom_call_target="tpu_custom_call" | custom-call | flops 10000000000 | bytes 10000000 | tf_op jit(solution)/shard_map/fetch/pallas_call | solution.py:279
  82.6 8.6 %collective-permute-done.8.refs_3_ = bf16[880,128]{1,0:T(8,128)(2,1)S(1)} collective-permute-done((bf16[880,128]{1,0:T(8,128)(2,1)S(1)}, bf16[880,128]{1,0:T(8,128)(2,1)S(1)}, u32[]{:S(2)}, u32[]{:S(2)}) %collective-permute-start.8) | collective-permute-done | bytes 225312 | tf_op jit(solution)/shard_map/ppermute | solution.py:509
  91.6 1.8 %collective-permute-start.10 = (bf16[48,1152]{1,0:T(8,128)(2,1)S(1)}, bf16[48,1152]{1,0:T(8,128)(2,1)S(1)}, u32[]{:S(2)}, u32[]{:S(2)}) collective-permute-start(bf16[48,1152]{1,0:T(8,128)(2,1)S(1)} %activate.1.refs_0_), channel_id=1, source_target_pairs={{0,64},{64,0},{128,192},{192,128},{1,65},{65,1},{129,193},{193,129... | collective-permute-start | bytes 331784 | tf_op jit(solution)/shard_map/ppermute | solution.py:509
  93.3 4.1 %collective-permute-done.11.refs_2_ = bf16[48,1152]{1,0:T(8,128)(2,1)S(1)} collective-permute-done((bf16[48,1152]{1,0:T(8,128)(2,1)S(1)}, bf16[48,1152]{1,0:T(8,128)(2,1)S(1)}, u32[]{:S(2)}, u32[]{:S(2)}) %collective-permute-start.11) | collective-permute-done | bytes 110624 | tf_op jit(solution)/shard_map/ppermute | solution.py:509
  97.7 1.5 %down_most.1.most_ref = bf16[384,896]{1,0:T(8,128)(2,1)S(1)} custom-call(s32[1]{0:T(128)} %bitcast.4.z_ref, bf16[48,1152]{1,0:T(8,128)(2,1)S(1)} %activate.1.refs_0_, bf16[48,1152]{1,0:T(8,128)(2,1)S(1)} %collective-permute-done.10.refs_1_, bf16[48,1152]{1,0:T(8,128)(2,1)S(1)} %collective-permute-done.11.refs_2_, ...), custom_call_target="tpu_custom_call" | custom-call | flops 10000000000 | bytes 10000000 | tf_op jit(solution)/shard_map/down_most/pallas_call | solution.py:235
  99.3 2.9 %collective-permute-done.12.rows_ref = bf16[48,1152]{1,0:T(8,128)(2,1)S(1)} collective-permute-done((bf16[48,1152]{1,0:T(8,128)(2,1)S(1)}, bf16[48,1152]{1,0:T(8,128)(2,1)S(1)}, u32[]{:S(2)}, u32[]{:S(2)}) %collective-permute-start.12) | collective-permute-done | bytes 110624 | tf_op jit(solution)/shard_map/ppermute | solution.py:509
  102.2 1.1 down.1
  103.3 14.2 %all_to_all.23.parts_ref = bf16[16,24,896]{2,1,0:T(8,128)(2,1)S(1)} all-to-all(bf16[16,24,896]{2,1,0:T(8,128)(2,1)S(1)} %bitcast.13), channel_id=1, replica_groups=mesh['z'=4,'core'=2,'x'=4,'y'=4,'rep'=2] {'x','y'}, dimensions={0} | all-to-all | bytes 1376256 | tf_op jit(solution)/shard_map/all_to_all | solution.py:590
  118.0 2.7 %collective-permute-start.14 = (bf16[8,896]{1,0:T(8,128)(2,1)S(1)}, bf16[8,896]{1,0:T(8,128)(2,1)S(1)}, u32[]{:S(2)}, u32[]{:S(2)}) collective-permute-start(bf16[8,896]{1,0:T(8,128)(2,1)S(1)} %get-tuple-element.81), channel_id=1, source_target_pairs={{0,128},{64,192},{128,0},{192,64},{1,129},{65,193},{129,1},{193,65... | collective-permute-start | bytes 43016 | tf_op jit(solution)/shard_map/ppermute | solution.py:509
  120.7 1.7 %collective-permute-start.15 = (bf16[8,896]{1,0:T(8,128)(2,1)S(1)}, bf16[8,896]{1,0:T(8,128)(2,1)S(1)}, u32[]{:S(2)}, u32[]{:S(2)}) collective-permute-start(bf16[8,896]{1,0:T(8,128)(2,1)S(1)} %get-tuple-element.82), channel_id=1, source_target_pairs={{0,192},{64,128},{128,64},{192,0},{1,193},{65,129},{129,65},{193,1... | collective-permute-start | bytes 43016 | tf_op jit(solution)/shard_map/ppermute | solution.py:509
  122.7 3.5 %collective-permute-done.15.refs_3_ = bf16[8,896]{1,0:T(8,128)(2,1)S(1)} collective-permute-done((bf16[8,896]{1,0:T(8,128)(2,1)S(1)}, bf16[8,896]{1,0:T(8,128)(2,1)S(1)}, u32[]{:S(2)}, u32[]{:S(2)}) %collective-permute-start.15) | collective-permute-done | bytes 14368 | tf_op jit(solution)/shard_map/ppermute | solution.py:509
  (41 shorter events, 4.8 us)
Async XLA Ops:
  0.0 30.3 %copy-start = (bf16[1024,896]{1,0:T(8,128)(2,1)S(1)}, bf16[1024,896]{1,0:T(8,128)(2,1)}, u32[]{:S(2)}) copy-start(bf16[1024,896]{1,0:T(8,128)(2,1)} %weight_ref.3) | copy-start | bytes 5505028
  30.2 1.1 copy-start.5
  30.2 1.8 %collective-permute-start = (bf16[192,1024]{1,0:T(8,128)(2,1)S(1)}, bf16[192,1024]{1,0:T(8,128)(2,1)S(1)}, u32[]{:S(2)}, u32[]{:S(2)}) collective-permute-start(bf16[192,1024]{1,0:T(8,128)(2,1)S(1)} %to_rows.1.rows_ref), channel_id=1, source_target_pairs={{0,32},{32,0},{1,33},{33,1},{2,34},{34,2},{3,35},{35,3},{4,36},{36... | collective-permute-start | bytes 1179656 | tf_op jit(solution)/shard_map/ppermute | solution.py:513
  31.3 18.5 %copy-start.1 = (bf16[3,128,896]{2,1,0:T(8,128)(2,1)S(1)}, bf16[3,128,896]{2,1,0:T(8,128)(2,1)}, u32[]{:S(2)}) copy-start(bf16[3,128,896]{2,1,0:T(8,128)(2,1)} %param.11) | copy-start | bytes 2064388
  33.0 32.8 %copy-start.2 = (bf16[896,1152]{1,0:T(8,128)(2,1)S(1)}, bf16[896,1152]{1,0:T(8,128)(2,1)}, u32[]{:S(2)}) copy-start(bf16[896,1152]{1,0:T(8,128)(2,1)} %gate_ref.3) | copy-start | bytes 6193156
  33.0 32.8 %copy-start.3 = (bf16[896,1152]{1,0:T(8,128)(2,1)S(1)}, bf16[896,1152]{1,0:T(8,128)(2,1)}, u32[]{:S(2)}) copy-start(bf16[896,1152]{1,0:T(8,128)(2,1)} %up_ref.3) | copy-start | bytes 6193156
  67.3 2.2 %collective-permute-start.3 = (bf16[16,896]{1,0:T(8,128)(2,1)S(1)}, bf16[16,896]{1,0:T(8,128)(2,1)S(1)}, u32[]{:S(2)}, u32[]{:S(2)}) collective-permute-start(bf16[16,896]{1,0:T(8,128)(2,1)S(1)} %get-tuple-element.59), channel_id=1, source_target_pairs={{0,32},{32,0},{1,33},{33,1},{2,34},{34,2},{3,35},{35,3},{4,36},{36... | collective-permute-start | bytes 86024 | tf_op jit(solution)/shard_map/ppermute | solution.py:513
  67.4 2.1 %collective-permute-start.1 = (bf16[880,128]{1,0:T(8,128)(2,1)S(1)}, bf16[880,128]{1,0:T(8,128)(2,1)S(1)}, u32[]{:S(2)}, u32[]{:S(2)}) collective-permute-start(bf16[880,128]{1,0:T(8,128)(2,1)S(1)} %get-tuple-element.54), channel_id=1, source_target_pairs={{0,32},{32,0},{1,33},{33,1},{2,34},{34,2},{3,35},{35,3},{4,36},{36... | collective-permute-start | bytes 675848 | tf_op jit(solution)/shard_map/ppermute | solution.py:513
  67.9 1.7 %copy-start.4 = (bf16[1152,896]{1,0:T(8,128)(2,1)S(1)}, bf16[1152,896]{1,0:T(8,128)(2,1)}, u32[]{:S(2)}) copy-start(bf16[1152,896]{1,0:T(8,128)(2,1)} %refs_0_) | copy-start | bytes 6193156
  67.9 1.6 %collective-permute-start.2 = (bf16[880,128]{1,0:T(8,128)(2,1)S(1)}, bf16[880,128]{1,0:T(8,128)(2,1)S(1)}, u32[]{:S(2)}, u32[]{:S(2)}) collective-permute-start(bf16[880,128]{1,0:T(8,128)(2,1)S(1)} %get-tuple-element.55), channel_id=1, source_target_pairs={{0,32},{32,0},{1,33},{33,1},{2,34},{34,2},{3,35},{35,3},{4,36},{36... | collective-permute-start | bytes 675848 | tf_op jit(solution)/shard_map/ppermute | solution.py:513
  69.6 10.1 %collective-permute-start.9 = (bf16[1152,896]{1,0:T(8,128)(2,1)S(1)}, bf16[1152,896]{1,0:T(8,128)(2,1)S(1)}, u32[]{:S(2)}, u32[]{:S(2)}) collective-permute-start(bf16[1152,896]{1,0:T(8,128)(2,1)S(1)} %copy-done.4), channel_id=1, source_target_pairs={{0,32},{32,0},{1,33},{33,1},{2,34},{34,2},{3,35},{35,3},{4,36},{36... | collective-permute-start | bytes 6193160 | tf_op jit(solution)/shard_map/ppermute | solution.py:513
  70.2 4.0 %collective-permute-start.6 = (bf16[880,128]{1,0:T(8,128)(2,1)S(1)}, bf16[880,128]{1,0:T(8,128)(2,1)S(1)}, u32[]{:S(2)}, u32[]{:S(2)}) collective-permute-start(bf16[880,128]{1,0:T(8,128)(2,1)S(1)} %get-tuple-element.69), channel_id=1, source_target_pairs={{0,32},{32,0},{1,33},{33,1},{2,34},{34,2},{3,35},{35,3},{4,36},{36... | collective-permute-start | bytes 675848 | tf_op jit(solution)/shard_map/ppermute | solution.py:513
  70.4 8.3 %collective-permute-start.7 = (bf16[880,128]{1,0:T(8,128)(2,1)S(1)}, bf16[880,128]{1,0:T(8,128)(2,1)S(1)}, u32[]{:S(2)}, u32[]{:S(2)}) collective-permute-start(bf16[880,128]{1,0:T(8,128)(2,1)S(1)} %add.7), channel_id=1, source_target_pairs={{0,64},{64,0},{128,192},{192,128},{1,65},{65,1},{129,193},{193,129... | collective-permute-start | bytes 675848 | tf_op jit(solution)/shard_map/ppermute | solution.py:509
  71.0 20.3 %collective-permute-start.5 = (bf16[880,128]{1,0:T(8,128)(2,1)S(1)}, bf16[880,128]{1,0:T(8,128)(2,1)S(1)}, u32[]{:S(2)}, u32[]{:S(2)}) collective-permute-start(bf16[880,128]{1,0:T(8,128)(2,1)S(1)} %add.8), channel_id=1, source_target_pairs={{0,64},{64,0},{128,192},{192,128},{1,65},{65,1},{129,193},{193,129... | collective-permute-start | bytes 675848 | tf_op jit(solution)/shard_map/ppermute | solution.py:509
  72.4 18.8 %collective-permute-start.4 = (bf16[880,128]{1,0:T(8,128)(2,1)S(1)}, bf16[880,128]{1,0:T(8,128)(2,1)S(1)}, u32[]{:S(2)}, u32[]{:S(2)}) collective-permute-start(bf16[880,128]{1,0:T(8,128)(2,1)S(1)} %get-tuple-element.65), channel_id=1, source_target_pairs={{0,32},{32,0},{1,33},{33,1},{2,34},{34,2},{3,35},{35,3},{4,36},{36... | collective-permute-start | bytes 675848 | tf_op jit(solution)/shard_map/ppermute | solution.py:513
  78.8 12.4 %collective-permute-start.8 = (bf16[880,128]{1,0:T(8,128)(2,1)S(1)}, bf16[880,128]{1,0:T(8,128)(2,1)S(1)}, u32[]{:S(2)}, u32[]{:S(2)}) collective-permute-start(bf16[880,128]{1,0:T(8,128)(2,1)S(1)} %add.9), channel_id=1, source_target_pairs={{0,128},{64,192},{128,0},{192,64},{1,129},{65,193},{129,1},{193,65... | collective-permute-start | bytes 675848 | tf_op jit(solution)/shard_map/ppermute | solution.py:509
  91.5 6.0 %collective-permute-start.11 = (bf16[48,1152]{1,0:T(8,128)(2,1)S(1)}, bf16[48,1152]{1,0:T(8,128)(2,1)S(1)}, u32[]{:S(2)}, u32[]{:S(2)}) collective-permute-start(bf16[48,1152]{1,0:T(8,128)(2,1)S(1)} %activate.1.refs_0_), channel_id=1, source_target_pairs={{0,128},{64,192},{128,0},{192,64},{1,129},{65,193},{129,1},{193,65... | collective-permute-start | bytes 331784 | tf_op jit(solution)/shard_map/ppermute | solution.py:509
  91.6 6.2 %collective-permute-start.10 = (bf16[48,1152]{1,0:T(8,128)(2,1)S(1)}, bf16[48,1152]{1,0:T(8,128)(2,1)S(1)}, u32[]{:S(2)}, u32[]{:S(2)}) collective-permute-start(bf16[48,1152]{1,0:T(8,128)(2,1)S(1)} %activate.1.refs_0_), channel_id=1, source_target_pairs={{0,64},{64,0},{128,192},{192,128},{1,65},{65,1},{129,193},{193,129... | collective-permute-start | bytes 331784 | tf_op jit(solution)/shard_map/ppermute | solution.py:509
  97.5 4.7 %collective-permute-start.12 = (bf16[48,1152]{1,0:T(8,128)(2,1)S(1)}, bf16[48,1152]{1,0:T(8,128)(2,1)S(1)}, u32[]{:S(2)}, u32[]{:S(2)}) collective-permute-start(bf16[48,1152]{1,0:T(8,128)(2,1)S(1)} %collective-permute-done.11.refs_2_), channel_id=1, source_target_pairs={{0,64},{64,0},{128,192},{192,128},{1,65},{65,1},{129,193},{193,129... | collective-permute-start | bytes 331784 | tf_op jit(solution)/shard_map/ppermute | solution.py:509
  117.9 4.5 %collective-permute-start.13 = (bf16[8,896]{1,0:T(8,128)(2,1)S(1)}, bf16[8,896]{1,0:T(8,128)(2,1)S(1)}, u32[]{:S(2)}, u32[]{:S(2)}) collective-permute-start(bf16[8,896]{1,0:T(8,128)(2,1)S(1)} %get-tuple-element.80), channel_id=1, source_target_pairs={{0,64},{64,0},{128,192},{192,128},{1,65},{65,1},{129,193},{193,129... | collective-permute-start | bytes 43016 | tf_op jit(solution)/shard_map/ppermute | solution.py:509
  118.0 4.7 %collective-permute-start.14 = (bf16[8,896]{1,0:T(8,128)(2,1)S(1)}, bf16[8,896]{1,0:T(8,128)(2,1)S(1)}, u32[]{:S(2)}, u32[]{:S(2)}) collective-permute-start(bf16[8,896]{1,0:T(8,128)(2,1)S(1)} %get-tuple-element.81), channel_id=1, source_target_pairs={{0,128},{64,192},{128,0},{192,64},{1,129},{65,193},{129,1},{193,65... | collective-permute-start | bytes 43016 | tf_op jit(solution)/shard_map/ppermute | solution.py:509
  120.7 5.5 %collective-permute-start.15 = (bf16[8,896]{1,0:T(8,128)(2,1)S(1)}, bf16[8,896]{1,0:T(8,128)(2,1)S(1)}, u32[]{:S(2)}, u32[]{:S(2)}) collective-permute-start(bf16[8,896]{1,0:T(8,128)(2,1)S(1)} %get-tuple-element.82), channel_id=1, source_target_pairs={{0,192},{64,128},{128,64},{192,0},{1,193},{65,129},{129,65},{193,1... | collective-permute-start | bytes 43016 | tf_op jit(solution)/shard_map/ppermute | solution.py:509

commit v5 on v3

--- a/solution.py
+++ b/solution.py
@@ -482,7 +482,7 @@
 
 
 def place_kernel(z_ref, core_ref, *refs):
-    *piece_refs, out_ref = refs
+    *piece_refs, out_ref, gathered = refs
     width = piece_refs[0].shape[1]
     micro = out_ref.shape[0]
     for k, ref in enumerate(piece_refs):
@@ -490,7 +490,8 @@
         for side in range(2):
             share = 2 * (z_ref[0] ^ k) + (core_ref[0] ^ side)
             at = pl.multiple_of(share * width, LANES)
-            out_ref[:, pl.ds(at, width)] = block[side * micro : (side + 1) * micro].astype(BF16)
+            gathered[:micro, pl.ds(at, width)] = block[side * micro : (side + 1) * micro]
+    out_ref[...] = gathered[:micro, :].astype(BF16)
 
 
 def place(z, core, pieces, micro):
@@ -500,6 +501,7 @@
         out_shape=jax.ShapeDtypeStruct((micro, 2 * len(pieces) * width), BF16),
         in_specs=[scalars(), scalars()] + [whole()] * len(pieces),
         out_specs=whole(),
+        scratch_shapes=[pltpu.VMEM((8, 2 * len(pieces) * width), F32)],
         compiler_params=params(8),
         name="place",
     )(z, core, *pieces)

time: 126 us -> 126 us (level)
  no operation moved by 1% of the time
where the time goes in v5:
time: 126 us
  blocking collectives  72.9 us (58%)
  waiting for transfers between devices  25.5 us (20%)
  Pallas kernels  16 us (13%)
  starting transfers between devices  11.1 us (9%)
    all_to_all x1, blocking collectives, per_device(): lax.all_to_all(payload, (Z,) + FFN, split_axis=0, concat_axis=0, tiled=True)  26.3 us
    ppermute x9, waiting for transfers between devices, along_z(): lax.ppermute(array, Z, [(i, i ^ hop) for i in range(lax.axis_size(Z))])  21.9 us
    all_to_all x1, blocking collectives, per_device(): lax.all_to_all(mixed.reshape(ffn_count, rows_chunk, col_share), FFN, spli...  16.8 us
    all_to_all x1, blocking collectives, per_device(): lax.all_to_all(copies, FFN, split_axis=0, concat_axis=0, tiled=True)  15.6 us
    all_to_all x1, blocking collectives, per_device(): lax.all_to_all(lowered.reshape(ffn_count, rows_chunk, col_share), FFN, sp...  14.2 us
    ppermute x9, starting transfers between devices, along_z(): lax.ppermute(array, Z, [(i, i ^ hop) for i in range(lax.axis_size(Z))])  9.73 us
    pallas_call x1, Pallas kernels, attend(): pl.pallas_call(attention_kernel, in_specs=[in_hbm()] * 5, out_specs=whole...  3.67 us
    ppermute x7, waiting for transfers between devices, swap_cores(): return lax.ppermute(array, CORE, [(0, 1), (1, 0)])  3.64 us
  transfers between devices with their start and end apart: 16, of which 9 were waited for; matrix products, arithmetic and copies ran while one was open for 0% of the time, Pallas kernels for 6%

profile of v5, /device:TPU:8, one launch (start us, length us, event | category | flops | bytes accessed | tf_op | source)
XLA Modules:
  0.0 125.8 jit_solution(4280222892619134516)
XLA Ops:
  0.0 3.7 %attention.1 = bf16[4,16,3,8,128]{4,3,2,1,0:T(8,128)(2,1)} custom-call(s32[1,3]{1,0:T(1,128)} %bitcast.21, s32[1,3]{1,0:T(1,128)} %bitcast.22, bf16[3,16384]{1,0:T(4,128)(2,1)} %bitcast.20, bf16[3,1024,256]{2,1,0:T(8,128)(2,1)} %key_hbm.1, bf16[3,1024,256]{2,1,0:T(8,128)(2,1)} %value_hbm.1), custom_call_target="tpu_custom_call" | custom-call | tf_op jit(solution)/shard_map/attention/pallas_call | solution.py:117
  3.7 26.3 %all_to_all.20 = bf16[64,24,128]{2,1,0:T(8,128)(2,1)S(1)} all-to-all(bf16[64,24,128]{2,1,0:T(8,128)(2,1)} %bitcast.19), channel_id=1, replica_groups=mesh['z'=4,'core'=2,'x'=4,'y'=4,'rep'=2] {'z','x','y'}, dimensions={0} | all-to-all | bytes 786432 | tf_op jit(solution)/shard_map/all_to_all | solution.py:553
  30.3 1.0 product.1.own_ref
  32.0 1.0 mix.1
  33.0 16.8 %all_to_all.21.parts_ref = bf16[16,24,896]{2,1,0:T(8,128)(2,1)S(1)} all-to-all(bf16[16,24,896]{2,1,0:T(8,128)(2,1)S(1)} %bitcast.14), channel_id=1, replica_groups=mesh['z'=4,'core'=2,'x'=4,'y'=4,'rep'=2] {'x','y'}, dimensions={0} | all-to-all | bytes 1376256 | tf_op jit(solution)/shard_map/all_to_all | solution.py:562
  50.2 15.6 %all_to_all.22 = bf16[16,24,896]{2,1,0:T(8,128)(2,1)S(1)} all-to-all(bf16[16,24,896]{2,1,0:T(8,128)(2,1)S(1)} %get-tuple-element.53), channel_id=1, replica_groups=mesh['z'=4,'core'=2,'x'=4,'y'=4,'rep'=2] {'x','y'}, dimensions={0} | all-to-all | bytes 1376256 | tf_op jit(solution)/shard_map/all_to_all | solution.py:566
  65.8 1.5 %up_part.2 = (bf16[880,128]{1,0:T(8,128)(2,1)S(1)}, bf16[880,128]{1,0:T(8,128)(2,1)S(1)}, bf16[880,128]{1,0:T(8,128)(2,1)S(1)}, bf16[880,128]{1,0:T(8,128)(2,1)S(1)}) custom-call(s32[1]{0:T(128)} %bitcast.4.z_ref, s32[1]{0:T(128)} %bitcast.5.core_ref, bf16[384,896]{1,0:T(8,128)(2,1)S(1)} %bitcast.17, bf16[1,896]{1,0:T(2,128)(2,1)S(1)} %broadcast_in_dim.15.gain_ref, ...), custom_call_target="tpu_custom_call" | custom-call | flops 10000000000 | bytes 10000000 | tf_op jit(solution)/shard_map/up_part/pallas_call | solution.py:379
  67.9 1.5 %up_part.3 = (bf16[880,128]{1,0:T(8,128)(2,1)S(1)}, bf16[880,128]{1,0:T(8,128)(2,1)S(1)}, bf16[880,128]{1,0:T(8,128)(2,1)S(1)}, bf16[880,128]{1,0:T(8,128)(2,1)S(1)}) custom-call(s32[1]{0:T(128)} %bitcast.4.z_ref, s32[1]{0:T(128)} %bitcast.5.core_ref, bf16[384,896]{1,0:T(8,128)(2,1)S(1)} %bitcast.18, bf16[1,896]{1,0:T(2,128)(2,1)S(1)} %broadcast_in_dim.15.gain_ref, ...), custom_call_target="tpu_custom_call" | custom-call | flops 10000000000 | bytes 10000000 | tf_op jit(solution)/shard_map/up_part/pallas_call | solution.py:379
  70.8 1.4 %collective-permute-start.4 = (bf16[880,128]{1,0:T(8,128)(2,1)S(1)}, bf16[880,128]{1,0:T(8,128)(2,1)S(1)}, u32[]{:S(2)}, u32[]{:S(2)}) collective-permute-start(bf16[880,128]{1,0:T(8,128)(2,1)S(1)} %add.8), channel_id=1, source_target_pairs={{0,64},{64,0},{128,192},{192,128},{1,65},{65,1},{129,193},{193,129... | collective-permute-start | bytes 675848 | tf_op jit(solution)/shard_map/ppermute | solution.py:511
  72.3 1.7 %collective-permute-done.5.refs_1_ = bf16[880,128]{1,0:T(8,128)(2,1)S(1)} collective-permute-done((bf16[880,128]{1,0:T(8,128)(2,1)S(1)}, bf16[880,128]{1,0:T(8,128)(2,1)S(1)}, u32[]{:S(2)}, u32[]{:S(2)}) %collective-permute-start.5) | collective-permute-done | bytes 225312 | tf_op jit(solution)/shard_map/ppermute | solution.py:515
  74.0 4.6 %collective-permute-done.6.refs_2_ = bf16[880,128]{1,0:T(8,128)(2,1)S(1)} collective-permute-done((bf16[880,128]{1,0:T(8,128)(2,1)S(1)}, bf16[880,128]{1,0:T(8,128)(2,1)S(1)}, u32[]{:S(2)}, u32[]{:S(2)}) %collective-permute-start.6) | collective-permute-done | bytes 225312 | tf_op jit(solution)/shard_map/ppermute | solution.py:511
  78.7 1.0 collective-permute-start.7
  79.7 2.8 %fetch.1 = (bf16[1152,896]{1,0:T(8,128)(2,1)S(1)}, bf16[1152,896]{1,0:T(8,128)(2,1)S(1)}) custom-call(bf16[1152,896]{1,0:T(8,128)(2,1)S(1)} %copy-done.4, bf16[1152,896]{1,0:T(8,128)(2,1)S(1)} %collective-permute-done.8.refs_1_), custom_call_target="tpu_custom_call" | custom-call | flops 10000000000 | bytes 10000000 | tf_op jit(solution)/shard_map/fetch/pallas_call | solution.py:279
  82.5 7.9 %collective-permute-done.7.refs_3_ = bf16[880,128]{1,0:T(8,128)(2,1)S(1)} collective-permute-done((bf16[880,128]{1,0:T(8,128)(2,1)S(1)}, bf16[880,128]{1,0:T(8,128)(2,1)S(1)}, u32[]{:S(2)}, u32[]{:S(2)}) %collective-permute-start.7) | collective-permute-done | bytes 225312 | tf_op jit(solution)/shard_map/ppermute | solution.py:511
  90.8 2.2 %collective-permute-start.9 = (bf16[48,1152]{1,0:T(8,128)(2,1)S(1)}, bf16[48,1152]{1,0:T(8,128)(2,1)S(1)}, u32[]{:S(2)}, u32[]{:S(2)}) collective-permute-start(bf16[48,1152]{1,0:T(8,128)(2,1)S(1)} %activate.1.refs_0_), channel_id=1, source_target_pairs={{0,64},{64,0},{128,192},{192,128},{1,65},{65,1},{129,193},{193,129... | collective-permute-start | bytes 331784 | tf_op jit(solution)/shard_map/ppermute | solution.py:511
  92.9 1.2 collective-permute-done.11.received_ref
  94.1 2.8 %collective-permute-done.10.refs_2_ = bf16[48,1152]{1,0:T(8,128)(2,1)S(1)} collective-permute-done((bf16[48,1152]{1,0:T(8,128)(2,1)S(1)}, bf16[48,1152]{1,0:T(8,128)(2,1)S(1)}, u32[]{:S(2)}, u32[]{:S(2)}) %collective-permute-start.10) | collective-permute-done | bytes 110624 | tf_op jit(solution)/shard_map/ppermute | solution.py:511
  96.9 1.5 %down_most.1.most_ref = bf16[384,896]{1,0:T(8,128)(2,1)S(1)} custom-call(s32[1]{0:T(128)} %bitcast.4.z_ref, bf16[48,1152]{1,0:T(8,128)(2,1)S(1)} %activate.1.refs_0_, bf16[48,1152]{1,0:T(8,128)(2,1)S(1)} %collective-permute-done.9.refs_1_, bf16[48,1152]{1,0:T(8,128)(2,1)S(1)} %collective-permute-done.10.refs_2_, ...), custom_call_target="tpu_custom_call" | custom-call | flops 10000000000 | bytes 10000000 | tf_op jit(solution)/shard_map/down_most/pallas_call | solution.py:235
  98.5 3.2 %collective-permute-done.12.rows_ref = bf16[48,1152]{1,0:T(8,128)(2,1)S(1)} collective-permute-done((bf16[48,1152]{1,0:T(8,128)(2,1)S(1)}, bf16[48,1152]{1,0:T(8,128)(2,1)S(1)}, u32[]{:S(2)}, u32[]{:S(2)}) %collective-permute-start.12) | collective-permute-done | bytes 110624 | tf_op jit(solution)/shard_map/ppermute | solution.py:511
  101.7 1.1 down.1
  102.8 14.2 %all_to_all.23.parts_ref = bf16[16,24,896]{2,1,0:T(8,128)(2,1)S(1)} all-to-all(bf16[16,24,896]{2,1,0:T(8,128)(2,1)S(1)} %bitcast.13), channel_id=1, replica_groups=mesh['z'=4,'core'=2,'x'=4,'y'=4,'rep'=2] {'x','y'}, dimensions={0} | all-to-all | bytes 1376256 | tf_op jit(solution)/shard_map/all_to_all | solution.py:591
  117.4 2.2 %collective-permute-start.14 = (bf16[8,896]{1,0:T(8,128)(2,1)S(1)}, bf16[8,896]{1,0:T(8,128)(2,1)S(1)}, u32[]{:S(2)}, u32[]{:S(2)}) collective-permute-start(bf16[8,896]{1,0:T(8,128)(2,1)S(1)} %get-tuple-element.83), channel_id=1, source_target_pairs={{0,128},{64,192},{128,0},{192,64},{1,129},{65,193},{129,1},{193,65... | collective-permute-start | bytes 43016 | tf_op jit(solution)/shard_map/ppermute | solution.py:511
  119.6 2.1 %collective-permute-start.15 = (bf16[8,896]{1,0:T(8,128)(2,1)S(1)}, bf16[8,896]{1,0:T(8,128)(2,1)S(1)}, u32[]{:S(2)}, u32[]{:S(2)}) collective-permute-start(bf16[8,896]{1,0:T(8,128)(2,1)S(1)} %get-tuple-element.84), channel_id=1, source_target_pairs={{0,192},{64,128},{128,64},{192,0},{1,193},{65,129},{129,65},{193,1... | collective-permute-start | bytes 43016 | tf_op jit(solution)/shard_map/ppermute | solution.py:511
  122.1 3.1 %collective-permute-done.15.refs_3_ = bf16[8,896]{1,0:T(8,128)(2,1)S(1)} collective-permute-done((bf16[8,896]{1,0:T(8,128)(2,1)S(1)}, bf16[8,896]{1,0:T(8,128)(2,1)S(1)}, u32[]{:S(2)}, u32[]{:S(2)}) %collective-permute-start.15) | collective-permute-done | bytes 14368 | tf_op jit(solution)/shard_map/ppermute | solution.py:511
  (41 shorter events, 5.1 us)
Async XLA Ops:
  0.0 30.3 %copy-start = (bf16[1024,896]{1,0:T(8,128)(2,1)S(1)}, bf16[1024,896]{1,0:T(8,128)(2,1)}, u32[]{:S(2)}) copy-start(bf16[1024,896]{1,0:T(8,128)(2,1)} %weight_ref.3) | copy-start | bytes 5505028
  30.2 1.1 copy-start.5
  30.2 1.8 %collective-permute-start = (bf16[192,1024]{1,0:T(8,128)(2,1)S(1)}, bf16[192,1024]{1,0:T(8,128)(2,1)S(1)}, u32[]{:S(2)}, u32[]{:S(2)}) collective-permute-start(bf16[192,1024]{1,0:T(8,128)(2,1)S(1)} %to_rows.1.rows_ref), channel_id=1, source_target_pairs={{0,32},{32,0},{1,33},{33,1},{2,34},{34,2},{3,35},{35,3},{4,36},{36... | collective-permute-start | bytes 1179656 | tf_op jit(solution)/shard_map/ppermute | solution.py:515
  31.3 18.5 %copy-start.1 = (bf16[3,128,896]{2,1,0:T(8,128)(2,1)S(1)}, bf16[3,128,896]{2,1,0:T(8,128)(2,1)}, u32[]{:S(2)}) copy-start(bf16[3,128,896]{2,1,0:T(8,128)(2,1)} %param.11) | copy-start | bytes 2064388
  33.0 32.8 %copy-start.2 = (bf16[896,1152]{1,0:T(8,128)(2,1)S(1)}, bf16[896,1152]{1,0:T(8,128)(2,1)}, u32[]{:S(2)}) copy-start(bf16[896,1152]{1,0:T(8,128)(2,1)} %gate_ref.3) | copy-start | bytes 6193156
  33.0 32.8 %copy-start.3 = (bf16[896,1152]{1,0:T(8,128)(2,1)S(1)}, bf16[896,1152]{1,0:T(8,128)(2,1)}, u32[]{:S(2)}) copy-start(bf16[896,1152]{1,0:T(8,128)(2,1)} %up_ref.3) | copy-start | bytes 6193156
  67.3 2.1 %collective-permute-start.1 = (bf16[880,128]{1,0:T(8,128)(2,1)S(1)}, bf16[880,128]{1,0:T(8,128)(2,1)S(1)}, u32[]{:S(2)}, u32[]{:S(2)}) collective-permute-start(bf16[880,128]{1,0:T(8,128)(2,1)S(1)} %get-tuple-element.55), channel_id=1, source_target_pairs={{0,32},{32,0},{1,33},{33,1},{2,34},{34,2},{3,35},{35,3},{4,36},{36... | collective-permute-start | bytes 675848 | tf_op jit(solution)/shard_map/ppermute | solution.py:515
  67.4 2.1 %copy-start.4 = (bf16[1152,896]{1,0:T(8,128)(2,1)S(1)}, bf16[1152,896]{1,0:T(8,128)(2,1)}, u32[]{:S(2)}) copy-start(bf16[1152,896]{1,0:T(8,128)(2,1)} %refs_0_) | copy-start | bytes 6193156
  67.4 2.0 %collective-permute-start.2 = (bf16[880,128]{1,0:T(8,128)(2,1)S(1)}, bf16[880,128]{1,0:T(8,128)(2,1)S(1)}, u32[]{:S(2)}, u32[]{:S(2)}) collective-permute-start(bf16[880,128]{1,0:T(8,128)(2,1)S(1)} %get-tuple-element.56), channel_id=1, source_target_pairs={{0,32},{32,0},{1,33},{33,1},{2,34},{34,2},{3,35},{35,3},{4,36},{36... | collective-permute-start | bytes 675848 | tf_op jit(solution)/shard_map/ppermute | solution.py:515
  69.5 10.2 %collective-permute-start.8 = (bf16[1152,896]{1,0:T(8,128)(2,1)S(1)}, bf16[1152,896]{1,0:T(8,128)(2,1)S(1)}, u32[]{:S(2)}, u32[]{:S(2)}) collective-permute-start(bf16[1152,896]{1,0:T(8,128)(2,1)S(1)} %copy-done.4), channel_id=1, source_target_pairs={{0,32},{32,0},{1,33},{33,1},{2,34},{34,2},{3,35},{35,3},{4,36},{36... | collective-permute-start | bytes 6193160 | tf_op jit(solution)/shard_map/ppermute | solution.py:515
  69.8 4.3 %collective-permute-start.5 = (bf16[880,128]{1,0:T(8,128)(2,1)S(1)}, bf16[880,128]{1,0:T(8,128)(2,1)S(1)}, u32[]{:S(2)}, u32[]{:S(2)}) collective-permute-start(bf16[880,128]{1,0:T(8,128)(2,1)S(1)} %get-tuple-element.67), channel_id=1, source_target_pairs={{0,32},{32,0},{1,33},{33,1},{2,34},{34,2},{3,35},{35,3},{4,36},{36... | collective-permute-start | bytes 675848 | tf_op jit(solution)/shard_map/ppermute | solution.py:515
  70.3 8.4 %collective-permute-start.6 = (bf16[880,128]{1,0:T(8,128)(2,1)S(1)}, bf16[880,128]{1,0:T(8,128)(2,1)S(1)}, u32[]{:S(2)}, u32[]{:S(2)}) collective-permute-start(bf16[880,128]{1,0:T(8,128)(2,1)S(1)} %add.7), channel_id=1, source_target_pairs={{0,64},{64,0},{128,192},{192,128},{1,65},{65,1},{129,193},{193,129... | collective-permute-start | bytes 675848 | tf_op jit(solution)/shard_map/ppermute | solution.py:511
  70.8 19.6 %collective-permute-start.4 = (bf16[880,128]{1,0:T(8,128)(2,1)S(1)}, bf16[880,128]{1,0:T(8,128)(2,1)S(1)}, u32[]{:S(2)}, u32[]{:S(2)}) collective-permute-start(bf16[880,128]{1,0:T(8,128)(2,1)S(1)} %add.8), channel_id=1, source_target_pairs={{0,64},{64,0},{128,192},{192,128},{1,65},{65,1},{129,193},{193,129... | collective-permute-start | bytes 675848 | tf_op jit(solution)/shard_map/ppermute | solution.py:511
  72.3 18.2 %collective-permute-start.3 = (bf16[880,128]{1,0:T(8,128)(2,1)S(1)}, bf16[880,128]{1,0:T(8,128)(2,1)S(1)}, u32[]{:S(2)}, u32[]{:S(2)}) collective-permute-start(bf16[880,128]{1,0:T(8,128)(2,1)S(1)} %get-tuple-element.63), channel_id=1, source_target_pairs={{0,32},{32,0},{1,33},{33,1},{2,34},{34,2},{3,35},{35,3},{4,36},{36... | collective-permute-start | bytes 675848 | tf_op jit(solution)/shard_map/ppermute | solution.py:515
  78.7 11.7 %collective-permute-start.7 = (bf16[880,128]{1,0:T(8,128)(2,1)S(1)}, bf16[880,128]{1,0:T(8,128)(2,1)S(1)}, u32[]{:S(2)}, u32[]{:S(2)}) collective-permute-start(bf16[880,128]{1,0:T(8,128)(2,1)S(1)} %add.9), channel_id=1, source_target_pairs={{0,128},{64,192},{128,0},{192,64},{1,129},{65,193},{129,1},{193,65... | collective-permute-start | bytes 675848 | tf_op jit(solution)/shard_map/ppermute | solution.py:511
  90.7 6.3 %collective-permute-start.10 = (bf16[48,1152]{1,0:T(8,128)(2,1)S(1)}, bf16[48,1152]{1,0:T(8,128)(2,1)S(1)}, u32[]{:S(2)}, u32[]{:S(2)}) collective-permute-start(bf16[48,1152]{1,0:T(8,128)(2,1)S(1)} %activate.1.refs_0_), channel_id=1, source_target_pairs={{0,128},{64,192},{128,0},{192,64},{1,129},{65,193},{129,1},{193,65... | collective-permute-start | bytes 331784 | tf_op jit(solution)/shard_map/ppermute | solution.py:511
  90.8 6.2 %collective-permute-start.9 = (bf16[48,1152]{1,0:T(8,128)(2,1)S(1)}, bf16[48,1152]{1,0:T(8,128)(2,1)S(1)}, u32[]{:S(2)}, u32[]{:S(2)}) collective-permute-start(bf16[48,1152]{1,0:T(8,128)(2,1)S(1)} %activate.1.refs_0_), channel_id=1, source_target_pairs={{0,64},{64,0},{128,192},{192,128},{1,65},{65,1},{129,193},{193,129... | collective-permute-start | bytes 331784 | tf_op jit(solution)/shard_map/ppermute | solution.py:511
  92.9 1.2 collective-permute-start.11
  96.9 4.7 %collective-permute-start.12 = (bf16[48,1152]{1,0:T(8,128)(2,1)S(1)}, bf16[48,1152]{1,0:T(8,128)(2,1)S(1)}, u32[]{:S(2)}, u32[]{:S(2)}) collective-permute-start(bf16[48,1152]{1,0:T(8,128)(2,1)S(1)} %collective-permute-done.10.refs_2_), channel_id=1, source_target_pairs={{0,64},{64,0},{128,192},{192,128},{1,65},{65,1},{129,193},{193,129... | collective-permute-start | bytes 331784 | tf_op jit(solution)/shard_map/ppermute | solution.py:511
  117.3 4.5 %collective-permute-start.13 = (bf16[8,896]{1,0:T(8,128)(2,1)S(1)}, bf16[8,896]{1,0:T(8,128)(2,1)S(1)}, u32[]{:S(2)}, u32[]{:S(2)}) collective-permute-start(bf16[8,896]{1,0:T(8,128)(2,1)S(1)} %get-tuple-element.82), channel_id=1, source_target_pairs={{0,64},{64,0},{128,192},{192,128},{1,65},{65,1},{129,193},{193,129... | collective-permute-start | bytes 43016 | tf_op jit(solution)/shard_map/ppermute | solution.py:511
  117.4 4.7 %collective-permute-start.14 = (bf16[8,896]{1,0:T(8,128)(2,1)S(1)}, bf16[8,896]{1,0:T(8,128)(2,1)S(1)}, u32[]{:S(2)}, u32[]{:S(2)}) collective-permute-start(bf16[8,896]{1,0:T(8,128)(2,1)S(1)} %get-tuple-element.83), channel_id=1, source_target_pairs={{0,128},{64,192},{128,0},{192,64},{1,129},{65,193},{129,1},{193,65... | collective-permute-start | bytes 43016 | tf_op jit(solution)/shard_map/ppermute | solution.py:511
  119.6 5.5 %collective-permute-start.15 = (bf16[8,896]{1,0:T(8,128)(2,1)S(1)}, bf16[8,896]{1,0:T(8,128)(2,1)S(1)}, u32[]{:S(2)}, u32[]{:S(2)}) collective-permute-start(bf16[8,896]{1,0:T(8,128)(2,1)S(1)} %get-tuple-element.84), channel_id=1, source_target_pairs={{0,192},{64,128},{128,64},{192,0},{1,193},{65,129},{129,65},{193,1... | collective-permute-start | bytes 43016 | tf_op jit(solution)/shard_map/ppermute | solution.py:511
